TPU v7x, 32 devices: a whole 2x2x4 slice. The times are simulated.
32 devices in a mesh: seq: 16 (over z, y, x), head: 2 (over core).
Axes of the slice: x: 2, y: 2, z: 4, core: 2. Of those that a mesh axis runs over, the one named last changes fastest.
Arguments:
- queries: bfloat16 [2048, 1024], P('seq', 'head'), may hold values from -6 to 6
- key_rows: bfloat16 [2048, 1024], P('seq', 'head'), may hold values from -6 to 6
- values: bfloat16 [2048, 2048], P('seq', 'head'), may hold values from -6 to 6
- out_gate: bfloat16 [2048, 2048], P('seq', 'head'), may hold values from -6 to 6
- write_rate: float32 [16, 2048], P('head', 'seq'), may hold values from 0 to 1
- log_decay: float32 [16, 2048], P('head', 'seq'), may hold values from -1 to 0, as said below
- norm_gain: float32 [128], replicated, may hold values from 0.1 to 1.9
- out_weight: bfloat16 [2048, 2048], P('head'), may hold values from -0.125 to 0.125
Outputs:
- layer_out: bfloat16 [2048, 2048], P('seq', 'head')
Inputs may be any that keep to these rules, and one draw needn't show every extreme that they name: `log_decay`: log decay of each value head and token, negative.
All inputs are finite; a program needn't handle non-finite values.
Results may differ from a plain program's by a relative error of at most 0.009.
Values may be sent and summed in bfloat16 or wider, within the bound.
No kernel may reach another device: no remote copies, remote signals or barrier semaphores. Data moves between devices by JAX's collectives and lax.ppermute only.
A program may use at most 320 MiB of HBM per device.

v0:
```python
import functools

import jax
import jax.numpy as jnp
from jax import lax
from jax.experimental import pallas as pl
from jax.experimental.pallas import tpu as pltpu
from jax.sharding import PartitionSpec as P

F32 = jnp.float32
BF16 = jnp.bfloat16
EPS = 1e-06
LEAF = 32
PAD = 16
SMALL = pltpu.CompilerParams(vmem_limit_bytes=24 * 1024 * 1024)


def dot(a, b):
    return jnp.dot(a.astype(BF16), b.astype(BF16), preferred_element_type=F32)


def dot_nt(a, b):
    return lax.dot_general(
        a.astype(BF16), b.astype(BF16), (((1,), (1,)), ((), ())), preferred_element_type=F32
    )


def dot_tn(a, b):
    return lax.dot_general(
        a.astype(BF16), b.astype(BF16), (((0,), (0,)), ((), ())), preferred_element_type=F32
    )


def exact_dot(a, b, dims):
    return lax.dot_general(
        a, b, (dims, ((), ())), precision=lax.Precision.HIGHEST, preferred_element_type=F32
    )


def parts(x):
    first = x.astype(BF16)
    rest = x - first.astype(F32)
    second = rest.astype(BF16)
    third = (rest - second.astype(F32)).astype(BF16)
    return [first, second, third]


def iota2(shape, dim):
    return lax.broadcasted_iota(jnp.int32, shape, dim)


def call(body, outs, specs, scratch=(), flops=0):
    return pl.pallas_call(
        body,
        out_shape=outs,
        in_specs=[pl.BlockSpec(memory_space=space) for space in specs],
        out_specs=jax.tree.map(lambda _: pl.BlockSpec(memory_space=pltpu.VMEM), outs),
        scratch_shapes=list(scratch),
        compiler_params=SMALL,
        cost_estimate=pl.CostEstimate(flops=flops, bytes_accessed=1 << 20, transcendentals=0),
    )


def unit_rows(x):
    return x * lax.rsqrt(jnp.sum(x * x, axis=-1, keepdims=True) + EPS)


def advance(keep, delta, feed, state):
    return keep * state - dot(delta, state) + feed


def join(late, early, whole=True):
    keep, delta, feed = late
    keep_e, delta_e, feed_e = early
    if not whole:
        return None, None, advance(keep, delta, feed, feed_e)
    dk = delta.shape[1]
    both = dot(delta, jnp.concatenate([delta_e, feed_e], axis=1))
    delta_new = keep * delta_e + keep_e * delta - both[:, 0:dk]
    return keep * keep_e, delta_new, keep * feed_e + feed - both[:, dk:]


def key_block(ref, col, dk):
    return unit_rows(ref[:, pl.ds(pl.multiple_of(col * dk, dk), dk)].astype(F32))


def slot_rows(ref, rank, slots, rep):
    return jnp.concatenate(
        [ref[pl.ds((rank ^ s) * rep + h, 1), :] for s in slots for h in range(rep)], axis=0
    )


def solve(lows, sides, i, j):
    tokens = i.shape[0]
    leaf = (i // LEAF) == (j // LEAF)
    unit = (i == j).astype(F32)
    power = [jnp.where(leaf, low, 0.0) for low in lows]
    inverse = [unit - p for p in power]
    power = [p.astype(BF16) for p in power]
    power = [dot(p, p).astype(BF16) for p in power]
    inverse = neumann(power, inverse, LEAF // 2, 1.0)
    both = [
        dot(t - unit, jnp.concatenate([jnp.where(leaf, 0.0, low), side], axis=1))
        for t, low, side in zip(inverse, lows, sides)
    ]
    power = [
        (jnp.where(leaf, 0.0, low) + b[:, 0:tokens]).astype(BF16) for low, b in zip(lows, both)
    ]
    sides = [side + b[:, tokens:] for side, b in zip(sides, both)]
    return neumann(power, sides, tokens // LEAF, -1.0)


def neumann(power, sides, order, sign):
    width = power[0].shape[1]
    reach = 1
    while 2 * reach < order:
        both = [
            dot(p, jnp.concatenate([p, s.astype(BF16)], axis=1)) for p, s in zip(power, sides)
        ]
        power = [b[:, 0:width].astype(BF16) for b in both]
        sides = [s + sign * b[:, width:] for s, b in zip(sides, both)]
        sign, reach = 1.0, 2 * reach
    return [s + sign * dot(p, s) for p, s in zip(power, sides)]


def tours(group):
    near = [s for s in range(1, group) if s.bit_count() == 1]
    far = sorted((s for s in range(1, group) if s.bit_count() > 1), key=lambda s: -s.bit_count())
    return [0] + far + near, [0] + far + near[::-1]


def flips(group, core):
    even, odd = tours(group)
    return [a if a == b else a + (b - a) * core for a, b in zip(even, odd)]


def placed(body, group):
    def run(*refs):
        index = lax.axis_index("seq")
        spot = (index & (group - 1), lax.axis_index("head"), index >> (group.bit_length() - 1))
        body(spot, *refs)

    return run


def pack_body(dk, dv, rep, group, where, k_in, v_in, rate_in, decay_in, *refs):
    slots = flips(group, where[1])
    *outs, rate_ref, decay_ref, sems = refs
    tokens = k_in.shape[0]
    rank = where[0]
    pairs = [(rate_in, rate_ref), (decay_in, decay_ref)]
    for s, out in zip(slots, outs):
        at = pl.multiple_of((rank ^ s) * dk, dk)
        pairs.append((k_in.at[:, pl.ds(at, dk)], out.at[0:tokens, :]))
        for h in range(rep):
            at = pl.multiple_of(((rank ^ s) * rep + h) * dv, dv)
            rows = out.at[(h + 1) * tokens : (h + 2) * tokens, :]
            pairs.append((v_in.at[:, pl.ds(at, dv)], rows))
    copies = [pltpu.make_async_copy(*p, sems.at[n]) for n, p in enumerate(pairs)]
    for copy in copies:
        copy.start()
    copies[0].wait()
    copies[1].wait()
    for s, out in zip(slots, outs):
        rows = [slot_rows(ref, rank, [s], rep) for ref in (rate_ref, decay_ref)]
        terms = [t.astype(F32) for t in parts(jnp.concatenate(rows, axis=0))]
        terms.append(jnp.zeros((PAD - 6 * rep, tokens), F32))
        out[(rep + 1) * tokens :, :] = jnp.concatenate(terms, axis=0).astype(BF16)
    for copy in copies[2:]:
        copy.wait()


def block_sides(decays, rates, tokens):
    i = iota2((tokens, tokens), 0)
    j = iota2((tokens, tokens), 1)
    lower = (i >= j).astype(F32)
    unit = (i == j).astype(F32)
    cum_rows = exact_dot(decays, lower, ((1,), (1,)))
    cum_cols = exact_dot(lower, decays, ((1,), (1,)))
    rate_cols = exact_dot(unit, rates, ((1,), (1,)))
    return i, j, cum_rows, cum_cols, rate_cols


def solve_blocks(keys, values, sides, rep):
    i, j, cum_rows, cum_cols, rate_cols = sides
    dots = [dot_nt(key, key) for key in keys]
    lows, rhs = [], []
    for n, value in enumerate(values):
        rate = rate_cols[:, n : n + 1]
        cum_col = cum_cols[:, n : n + 1]
        gap = cum_col - cum_rows[n : n + 1, :]
        lows.append(jnp.where(i > j, (rate * dots[n // rep]) * jnp.exp(gap), 0.0))
        rhs.append(
            jnp.concatenate([(rate * jnp.exp(cum_col)) * keys[n // rep], rate * value], axis=1)
        )
    return solve(lows, rhs, i, j)


def owner_body(dk, dv, rep, group, whole, where, *refs):
    slots = flips(group, where[1])
    *packs, _, send_ref, delta_ref, feed_ref, keep_ref, scr = refs
    blocks = len(packs)
    tokens = (packs[0].shape[0] - PAD) // (rep + 1)
    for s, pack in zip(slots, packs):
        scr[where[0] ^ s] = pack[...]
    tails = [scr[c, (rep + 1) * tokens :, :].astype(F32) for c in range(blocks)]
    size = 2 * rep
    tails = [t[0:size] + t[size : 2 * size] + t[2 * size : 3 * size] for t in tails]
    rates = jnp.concatenate([t[0:rep] for t in tails], axis=0)
    decays = jnp.concatenate([t[rep:] for t in tails], axis=0)
    sides = block_sides(decays, rates, tokens)
    cum_rows, cum_cols = sides[2], sides[3]
    keys = [unit_rows(scr[c, 0:tokens, :].astype(F32)) for c in range(blocks)]
    jobs = [(c, h) for c in range(blocks) for h in range(rep)]
    values = [scr[c, (h + 1) * tokens : (h + 2) * tokens, :].astype(F32) for c, h in jobs]
    solved = solve_blocks(keys, values, sides, rep)
    entries = []
    for n, (c, h) in enumerate(jobs):
        last = cum_rows[n : n + 1, tokens - 1 : tokens]
        moved = dot_tn(keys[c] * jnp.exp(last - cum_cols[:, n : n + 1]), solved[n])
        entries.append((jnp.exp(last), moved[:, 0:dk], moved[:, dk:]))
        delta_ref[n] = moved[:, 0:dk].astype(BF16)
        feed_ref[n] = moved[:, dk:]
        keep_ref[n : n + 1, :] = jnp.broadcast_to(jnp.exp(last), (1, keep_ref.shape[1]))
    store_send(send_ref, [fold(entries[h::rep], whole) for h in range(rep)], whole)


def fold(maps, whole):
    while len(maps) > 1:
        maps = [join(maps[n + 1], maps[n], whole or n > 0) for n in range(0, len(maps), 2)]
    return maps[0]


def block_maps(delta_ref, feed_ref, keep_ref, rep):
    maps = [
        (keep_ref[n : n + 1, 0:1], delta_ref[n].astype(F32), feed_ref[n])
        for n in range(delta_ref.shape[0])
    ]
    return [maps[h::rep] for h in range(rep)]


def terms_body(dk, dv, rep, group, where, q_in, k_in, v_in, rate_in, decay_in, *refs):
    slots = flips(group, where[1])
    x_ref, y_ref, q_ref, k_ref, v_ref, rate_ref, decay_ref, sems = refs
    tokens = k_in.shape[0]
    rank = where[0]
    pairs = [(rate_in, rate_ref), (decay_in, decay_ref), (k_in, k_ref), (v_in, v_ref), (q_in, q_ref)]
    copies = [pltpu.make_async_copy(*p, sems.at[n]) for n, p in enumerate(pairs)]
    for copy in copies:
        copy.start()
    copies[0].wait()
    copies[1].wait()
    sides = block_sides(
        slot_rows(decay_ref, rank, slots, rep), slot_rows(rate_ref, rank, slots, rep), tokens
    )
    i, j, cum_rows, cum_cols, _ = sides
    copies[2].wait()
    keys = [key_block(k_ref, rank ^ s, dk) for s in slots]
    copies[3].wait()
    values = []
    for n in range(len(slots) * rep):
        at = pl.multiple_of(((rank ^ slots[n // rep]) * rep + n % rep) * dv, dv)
        values.append(v_ref[:, pl.ds(at, dv)].astype(F32))
    solved = solve_blocks(keys, values, sides, rep)
    copies[4].wait()
    queries = [key_block(q_ref, rank ^ s, dk) * dk**-0.5 for s in slots]
    dots = [dot_nt(query, key) for query, key in zip(queries, keys)]
    for n in range(len(slots) * rep):
        cum_col = cum_cols[:, n : n + 1]
        gap = cum_col - cum_rows[n : n + 1, :]
        scores = jnp.where(i >= j, dots[n // rep] * jnp.exp(gap), 0.0)
        inner = dot(scores, solved[n])
        x_ref[n] = (queries[n // rep] * jnp.exp(cum_col) - inner[:, 0:dk]).astype(BF16)
        y_ref[n] = inner[:, dk:]


def store_maps(ref, entries):
    dk = entries[0][1].shape[0]
    for h, (_, delta, feed) in enumerate(entries):
        rows = slice(h * dk, (h + 1) * dk)
        ref[rows, 0:dk] = delta.astype(BF16)
        ref[rows, dk:] = feed.astype(BF16)
    width = ref.shape[1]
    rows = [jnp.broadcast_to(t.astype(F32), (1, width)) for e in entries for t in parts(e[0])]
    rows.append(jnp.zeros((PAD - len(rows), width), F32))
    ref[len(entries) * dk :, :] = jnp.concatenate(rows, axis=0).astype(BF16)


def load_maps(ref, dk, rep):
    tail = ref[rep * dk :, 0:dk].astype(F32)
    out = []
    for h in range(rep):
        keep = (tail[3 * h : 3 * h + 1] + tail[3 * h + 1 : 3 * h + 2]) + tail[3 * h + 2 : 3 * h + 3]
        rows = slice(h * dk, (h + 1) * dk)
        out.append((keep[:, 0:1], ref[rows, 0:dk].astype(F32), ref[rows, dk:].astype(F32)))
    return out


def pick(flag, yes, no):
    return [tuple(jnp.where(flag == 1, a, b) for a, b in zip(y, n)) for y, n in zip(yes, no)]


def store_send(ref, entries, whole):
    if whole:
        store_maps(ref, entries)
        return
    for h, (_, _, feed) in enumerate(entries):
        ref[h * feed.shape[0] : (h + 1) * feed.shape[0], :] = feed.astype(BF16)


def block_body(dk, rep, step, whole, where, own_ref, came_ref, out_ref):
    own, came = load_maps(own_ref, dk, rep), load_maps(came_ref, dk, rep)
    flag = (where[2] >> step) & 1
    late, early = pick(flag, own, came), pick(flag, came, own)
    store_send(out_ref, [join(l, e, whole) for l, e in zip(late, early)], whole)


def block_entry(dk, rep, group, *came):
    none = jnp.zeros((dk, dk), F32)
    entry = [(jnp.ones((1, 1), F32), none, none) for _ in range(rep)]
    for step, ref in enumerate(came):
        block = load_maps(ref, dk, rep)
        if step > 0:
            block = [join(l, e) for l, e in zip(entry, block)]
        entry = pick((group >> step) & 1, block, entry)
    return entry


def prefix_body(dk, rep, where, delta_ref, feed_ref, keep_ref, *refs):
    *came, a_ref, b_ref = refs
    maps = block_maps(delta_ref, feed_ref, keep_ref, rep)
    unit = (iota2((dk, dk), 0) == iota2((dk, dk), 1)).astype(F32)
    none = jnp.zeros((dk, dk), F32)
    entry = block_entry(dk, rep, where[2], *came)
    states = [jnp.concatenate([k * unit - d, f], axis=1) for k, d, f in entry]
    for c in range(a_ref.shape[0]):
        for h in range(rep):
            a_ref[c, h] = states[h][:, 0:dk].astype(BF16)
            b_ref[c, h] = states[h][:, dk:]
            keep, delta, feed = maps[h][c]
            if c + 1 < a_ref.shape[0]:
                feed = jnp.concatenate([none, feed], axis=1)
                states[h] = advance(keep, delta, feed, states[h])


def enter_body(dk, rep, group, steps, where, a_ref, b_ref, feed_ref, *outs):
    slots = flips(group, where[1])
    late = (where[2] >> (steps - 1)) & 1 if steps else 0
    feed = jnp.where(late == 1, feed_ref[...].astype(F32), 0.0).astype(BF16)
    for s, out in zip(slots, outs):
        for h in range(rep):
            rows = slice(h * dk, (h + 1) * dk)
            at = where[0] ^ s
            out[rows, :] = (dot(a_ref[at, h], feed[rows]) + b_ref[at, h]).astype(BF16)


def project_body(dk, dv, rep, group, at, where, x_ref, y_ref, gate_ref, gain_ref, w_ref, state, *refs):
    slots = flips(group, where[1])
    *before, out_ref, normed_ref = refs
    own = (where[0] ^ slots[at]) * rep
    outs = []
    for h in range(rep):
        n = at * rep + h
        outs.append(dot(x_ref[n], state[h * dk : (h + 1) * dk, :]) + y_ref[n])
    scaled, scales = [], []
    for h, o in enumerate(outs):
        gate = gate_ref[:, pl.ds(pl.multiple_of((own + h) * dv, dv), dv)].astype(F32)
        scales.append(lax.rsqrt(jnp.mean(o * o, axis=-1, keepdims=True) + EPS))
        scaled.append(o * (gain_ref[...] * (gate / (1.0 + jnp.exp(-gate)))))
        normed_ref[:, h * dv : (h + 1) * dv] = (scaled[h] * scales[h]).astype(BF16)
    columns = out_ref.shape[1]
    start = (1 - where[1]) * columns
    step = 256
    for n in range(columns // step):
        at = pl.multiple_of(start + n * step, step)
        cut = slice(n * step, (n + 1) * step)
        total = before[0][:, cut] if before else 0.0
        for h, (piece, scale) in enumerate(zip(scaled, scales)):
            rows = pl.ds(pl.multiple_of((own + h) * dv, dv), dv)
            total = total + scale * dot(piece, w_ref[rows, pl.ds(at, step)])
        out_ref[:, cut] = total.astype(out_ref.dtype)


def own_body(group, where, w_ref, *refs):
    slots = flips(group, where[1])
    *pieces, out_ref = refs
    columns = out_ref.shape[1]
    start = where[1] * columns
    width = pieces[0].shape[1]
    step = 256
    for n in range(columns // step):
        at = pl.multiple_of(start + n * step, step)
        total = 0.0
        for s, piece in zip(slots, pieces):
            rows = pl.ds(pl.multiple_of((where[0] ^ s) * width, width), width)
            total = total + dot(piece[...], w_ref[rows, pl.ds(at, step)])
        out_ref[:, n * step : (n + 1) * step] = total


def per_device(queries, key_rows, values, out_gate, write_rate, log_decay, norm_gain, out_weight):
    tokens = queries.shape[0]
    heads = write_rate.shape[0]
    dv = norm_gain.shape[0]
    dk = dv
    group = queries.shape[1] // dk
    rep = heads // group
    ranks = lax.axis_size("seq")
    halves = lax.axis_size("head")
    groups = ranks // group
    assert ranks % group == 0 and halves == 2
    assert group & (group - 1) == 0 and groups & (groups - 1) == 0
    steps = groups.bit_length() - 1
    columns = out_weight.shape[1] // halves
    shape = jax.ShapeDtypeStruct
    vmem, hbm = pltpu.VMEM, pltpu.HBM
    cube = 2 * tokens * tokens * (dk + dv)
    map_shape = shape((rep * dk + PAD, dk + dv), BF16)
    feed_shape = shape((rep * dk, dv), BF16)

    def swap(x, flip):
        return lax.ppermute(x, "seq", [(i, i ^ flip) for i in range(ranks)])

    def swap_slots(made):
        came = [made[0]]
        for x, *flip in list(zip(made, *tours(group)))[1:]:
            pairs = [(i * halves + c, (i ^ flip[c]) * halves + c) for i in range(ranks) for c in (0, 1)]
            came.append(lax.ppermute(x, ("seq", "head"), pairs))
        return came

    q_in, k_in, v_in, rate_in, decay_in = [
        pltpu.with_memory_space_constraint(x, hbm)
        for x in (queries, key_rows, values, write_rate, log_decay)
    ]
    small = [pltpu.VMEM(write_rate.shape, F32), pltpu.VMEM(log_decay.shape, F32)]
    pack_shape = shape(((rep + 1) * tokens + PAD, dk), BF16)
    packs = call(
        placed(functools.partial(pack_body, dk, dv, rep, group), group),
        [pack_shape] * group,
        [hbm] * 4,
        small + [pltpu.SemaphoreType.DMA((2 + (rep + 1) * group,))],
    )(k_in, v_in, rate_in, decay_in)
    packs = swap_slots(packs)
    x, y = call(
        placed(functools.partial(terms_body, dk, dv, rep, group), group),
        [shape((heads, tokens, dk), BF16), shape((heads, tokens, dv), F32)],
        [hbm] * 5,
        [pltpu.VMEM(z.shape, BF16) for z in (queries, key_rows, values)]
        + small
        + [pltpu.SemaphoreType.DMA((5,))],
        heads * 16 * cube,
    )(q_in, k_in, v_in, rate_in, decay_in)
    jobs = group * rep
    send, *blocks = call(
        placed(functools.partial(owner_body, dk, dv, rep, group, steps > 1), group),
        [
            map_shape if steps > 1 else feed_shape,
            shape((jobs, dk, dk), BF16),
            shape((jobs, dk, dv), F32),
            shape((jobs, dk), F32),
        ],
        [vmem] * group + [pl.ANY],
        [pltpu.VMEM((group,) + pack_shape.shape, BF16)],
        jobs * 16 * cube,
    )(*packs, y)

    came, feed = [], send
    for step in range(steps):
        got = swap(send, group << step)
        if step == steps - 1:
            feed = got
            continue
        whole = step + 2 < steps
        send = call(
            placed(functools.partial(block_body, dk, rep, step, whole), group),
            map_shape if whole else feed_shape,
            [vmem] * 2,
        )(send, got)
        came.append(got)
    a, b = call(
        placed(functools.partial(prefix_body, dk, rep), group),
        [shape((group, rep, dk, dk), BF16), shape((group, rep, dk, dv), F32)],
        [vmem] * (3 + len(came)),
        (),
        jobs * 4 * cube,
    )(*blocks, *came)
    states = call(
        placed(functools.partial(enter_body, dk, rep, group, steps), group),
        [feed_shape] * group,
        [vmem] * 3,
        (),
        cube * jobs,
    )(a, b, feed)
    states = swap_slots(states)

    work = 2 * tokens * columns * heads * dv
    away, normed = [], []
    for n, state in enumerate(states):
        kind = F32 if n < group - 1 else BF16
        total, piece = call(
            placed(functools.partial(project_body, dk, dv, rep, group, n), group),
            [shape((tokens, columns), kind), shape((tokens, rep * dv), BF16)],
            [vmem] * (6 + len(away)),
            (),
            work // group,
        )(x, y, out_gate, norm_gain.reshape(1, dv), out_weight, state, *away)
        away = [total]
        normed.append(piece)
    came = lax.ppermute(away[0], "head", [(0, 1), (1, 0)])
    own = call(placed(functools.partial(own_body, group), group), shape((tokens, columns), F32), [vmem] * (1 + group), (), work)(
        out_weight, *normed
    )
    return (own + came.astype(F32)).astype(BF16)


def solution(mesh):
    return jax.shard_map(
        per_device,
        mesh=mesh,
        in_specs=(
            P("seq", "head"),
            P("seq", "head"),
            P("seq", "head"),
            P("seq", "head"),
            P("head", "seq"),
            P("head", "seq"),
            P(),
            P("head", None),
        ),
        out_specs=P("seq", "head"),
        check_vma=False,
    )
```

profile of v0, /device:TPU:0, one launch (start us, length us, event | category | flops | bytes accessed | tf_op | source)
XLA Modules:
  0.0 34.2 jit_solution(12385179003621880277)
XLA Ops:
  0.0 1.1 %shard_map.83 = (bf16[400,128]{1,0:T(8,128)(2,1)S(1)}, bf16[400,128]{1,0:T(8,128)(2,1)S(1)}, bf16[400,128]{1,0:T(8,128)(2,1)S(1)}, bf16[400,128]{1,0:T(8,128)(2,1)S(1)}) custom-call(bf16[128,512]{1,0:T(8,128)(2,1)} %refs_0_.4, bf16[128,1024]{1,0:T(8,128)(2,1)} %refs_1_.3, f32[8,128]{1,0:T(8,128)} %refs_2_.7, f32[8,128]{1,0:T(8,128)} %refs_3_.3), custom_call_target="tpu_custom_call" | custom-call | bytes 1048576 | tf_op jit(solution)/shard_map/pallas_call | solution.py:436
  1.1 4.0 %collective-permute-start = (bf16[400,128]{1,0:T(8,128)(2,1)S(1)}, bf16[400,128]{1,0:T(8,128)(2,1)S(1)}, u32[]{:S(2)}, u32[]{:S(2)}) collective-permute-start(bf16[400,128]{1,0:T(8,128)(2,1)S(1)} %get-tuple-element.32), channel_id=1, source_target_pairs={{0,6},{1,7},{2,4},{3,5},{4,2},{5,3},{6,0},{7,1},{8,14},{9,15},{10,... | collective-permute-start | bytes 307208 | tf_op jit(solution)/shard_map/ppermute | solution.py:427
  5.1 0.5 %collective-permute-start.1 = (bf16[400,128]{1,0:T(8,128)(2,1)S(1)}, bf16[400,128]{1,0:T(8,128)(2,1)S(1)}, u32[]{:S(2)}, u32[]{:S(2)}) collective-permute-start(bf16[400,128]{1,0:T(8,128)(2,1)S(1)} %get-tuple-element.33), channel_id=1, source_target_pairs={{0,2},{1,5},{2,0},{3,7},{4,6},{5,1},{6,4},{7,3},{8,10},{9,13},{10,... | collective-permute-start | bytes 307208 | tf_op jit(solution)/shard_map/ppermute | solution.py:427
  5.6 0.0 copy-start
  5.6 0.0 copy-start.1
  5.6 0.0 copy-start.2
  5.6 0.1 collective-permute-start.2
  5.7 3.8 %shard_map.82 = (bf16[8,128,128]{2,1,0:T(8,128)(2,1)S(1)}, f32[8,128,128]{2,1,0:T(8,128)S(1)}) custom-call(bf16[128,512]{1,0:T(8,128)(2,1)} %refs_0_.3, bf16[128,512]{1,0:T(8,128)(2,1)} %refs_0_.4, bf16[128,1024]{1,0:T(8,128)(2,1)} %refs_1_.3, f32[8,128]{1,0:T(8,128)} %refs_2_.7, f32[8,128]{1,0:T(8,128)} %refs_3_.3), custom_call_target="tpu_custom_call" | custom-call | flops 1073741824 | bytes 1048576 | tf_op jit(solution)/shard_map/pallas_call | solution.py:443
  9.5 0.0 collective-permute-done.refs_1_
  9.5 0.9 %collective-permute-done.1.refs_2_ = bf16[400,128]{1,0:T(8,128)(2,1)S(1)} collective-permute-done((bf16[400,128]{1,0:T(8,128)(2,1)S(1)}, bf16[400,128]{1,0:T(8,128)(2,1)S(1)}, u32[]{:S(2)}, u32[]{:S(2)}) %collective-permute-start.1) | collective-permute-done | bytes 102432 | tf_op jit(solution)/shard_map/ppermute | solution.py:427
  10.4 0.0 collective-permute-done.2.refs_3_
  10.4 2.6 %shard_map.84 = (bf16[272,256]{1,0:T(8,128)(2,1)S(1)}, bf16[8,128,128]{2,1,0:T(8,128)(2,1)S(1)}, f32[8,128,128]{2,1,0:T(8,128)S(1)}, f32[8,128]{1,0:T(8,128)S(1)}) custom-call(bf16[400,128]{1,0:T(8,128)(2,1)S(1)} %get-tuple-element.31.refs_0_, bf16[400,128]{1,0:T(8,128)(2,1)S(1)} %collective-permute-done.refs_1_, ...), custom_call_target="tpu_custom_call" | custom-call | flops 1073741824 | bytes 1048576 | tf_op jit(solution)/shard_map/pallas_call | solution.py:453
  13.0 1.6 %collective-permute-start.3 = (bf16[272,256]{1,0:T(8,128)(2,1)S(1)}, bf16[272,256]{1,0:T(8,128)(2,1)S(1)}, u32[]{:S(2)}, u32[]{:S(2)}) collective-permute-start(bf16[272,256]{1,0:T(8,128)(2,1)S(1)} %get-tuple-element.38.refs_0_), channel_id=1, source_target_pairs={{0,8},{2,10},{4,12},{6,14},{8,0},{10,2},{12,4},{14,6},{16,24},{18,... | collective-permute-start | bytes 417800 | tf_op jit(solution)/shard_map/ppermute | solution.py:421
  14.7 3.5 %collective-permute-done.3.refs_3_.refs_1_ = bf16[272,256]{1,0:T(8,128)(2,1)S(1)} collective-permute-done((bf16[272,256]{1,0:T(8,128)(2,1)S(1)}, bf16[272,256]{1,0:T(8,128)(2,1)S(1)}, u32[]{:S(2)}, u32[]{:S(2)}) %collective-permute-start.3) | collective-permute-done | bytes 139296 | tf_op jit(solution)/shard_map/ppermute | solution.py:421
  18.1 0.2 shard_map.86
  18.3 2.7 %collective-permute-start.4 = (bf16[256,128]{1,0:T(8,128)(2,1)S(1)}, bf16[256,128]{1,0:T(8,128)(2,1)S(1)}, u32[]{:S(2)}, u32[]{:S(2)}) collective-permute-start(bf16[256,128]{1,0:T(8,128)(2,1)S(1)} %shard_map.86), channel_id=1, source_target_pairs={{0,16},{2,18},{4,20},{6,22},{8,24},{10,26},{12,28},{14,30},{16,0},... | collective-permute-start | bytes 196616 | tf_op jit(solution)/shard_map/ppermute | solution.py:421
  21.0 0.5 %shard_map.85 = (bf16[4,2,128,128]{3,2,1,0:T(8,128)(2,1)S(1)}, f32[4,2,128,128]{3,2,1,0:T(8,128)S(1)}) custom-call(bf16[8,128,128]{2,1,0:T(8,128)(2,1)S(1)} %get-tuple-element.35.refs_0_, f32[8,128,128]{2,1,0:T(8,128)S(1)} %get-tuple-element.36.refs_1_, f32[8,128]{1,0:T(8,128)S(1)} %get-tuple-element.37.refs_2_, ...), custom_call_target="tpu_custom_call" | custom-call | flops 268435456 | bytes 1048576 | tf_op jit(solution)/shard_map/pallas_call | solution.py:479
  21.5 2.0 %collective-permute-done.4.refs_2_ = bf16[256,128]{1,0:T(8,128)(2,1)S(1)} collective-permute-done((bf16[256,128]{1,0:T(8,128)(2,1)S(1)}, bf16[256,128]{1,0:T(8,128)(2,1)S(1)}, u32[]{:S(2)}, u32[]{:S(2)}) %collective-permute-start.4) | collective-permute-done | bytes 65568 | tf_op jit(solution)/shard_map/ppermute | solution.py:421
  23.6 0.2 shard_map.87
  23.8 1.9 %collective-permute-start.5 = (bf16[256,128]{1,0:T(8,128)(2,1)S(1)}, bf16[256,128]{1,0:T(8,128)(2,1)S(1)}, u32[]{:S(2)}, u32[]{:S(2)}) collective-permute-start(bf16[256,128]{1,0:T(8,128)(2,1)S(1)} %get-tuple-element.43), channel_id=1, source_target_pairs={{0,6},{1,7},{2,4},{3,5},{4,2},{5,3},{6,0},{7,1},{8,14},{9,15},{10,... | collective-permute-start | bytes 196616 | tf_op jit(solution)/shard_map/ppermute | solution.py:427
  25.7 1.5 %collective-permute-start.6 = (bf16[256,128]{1,0:T(8,128)(2,1)S(1)}, bf16[256,128]{1,0:T(8,128)(2,1)S(1)}, u32[]{:S(2)}, u32[]{:S(2)}) collective-permute-start(bf16[256,128]{1,0:T(8,128)(2,1)S(1)} %get-tuple-element.46), channel_id=1, source_target_pairs={{0,2},{1,5},{2,0},{3,7},{4,6},{5,1},{6,4},{7,3},{8,10},{9,13},{10,... | collective-permute-start | bytes 196616 | tf_op jit(solution)/shard_map/ppermute | solution.py:427
  27.2 0.2 collective-permute-start.7
  27.3 0.0 copy-done
  27.3 0.0 copy-done.1
  27.3 0.0 copy-done.2
  27.3 0.4 %shard_map.88 = (f32[128,1024]{1,0:T(8,128)S(1)}, bf16[128,256]{1,0:T(8,128)(2,1)S(1)}) custom-call(bf16[8,128,128]{2,1,0:T(8,128)(2,1)S(1)} %get-tuple-element.29.refs_0_, f32[8,128,128]{2,1,0:T(8,128)S(1)} %get-tuple-element.30.refs_4_.refs_1_, bf16[128,1024]{1,0:T(8,128)(2,1)S(1)} %copy-done.1, f32[1,128]{1,0:T(1,128)S(1)} %bitcast.1, ...), custom_call_target="tpu_custom_call" | custom-call | flops 67108864 | bytes 1048576 | tf_op jit(solution)/shard_map/pallas_call | solution.py:499
  27.8 1.2 %collective-permute-done.5.refs_5_ = bf16[256,128]{1,0:T(8,128)(2,1)S(1)} collective-permute-done((bf16[256,128]{1,0:T(8,128)(2,1)S(1)}, bf16[256,128]{1,0:T(8,128)(2,1)S(1)}, u32[]{:S(2)}, u32[]{:S(2)}) %collective-permute-start.5) | collective-permute-done | bytes 65568 | tf_op jit(solution)/shard_map/ppermute | solution.py:427
  29.0 0.4 %shard_map.89 = (f32[128,1024]{1,0:T(8,128)S(1)}, bf16[128,256]{1,0:T(8,128)(2,1)S(1)}) custom-call(bf16[8,128,128]{2,1,0:T(8,128)(2,1)S(1)} %get-tuple-element.29.refs_0_, f32[8,128,128]{2,1,0:T(8,128)S(1)} %get-tuple-element.30.refs_4_.refs_1_, bf16[128,1024]{1,0:T(8,128)(2,1)S(1)} %copy-done.1, f32[1,128]{1,0:T(1,128)S(1)} %bitcast.2, ...), custom_call_target="tpu_custom_call" | custom-call | flops 67108864 | bytes 1048576 | tf_op jit(solution)/shard_map/pallas_call | solution.py:499
  29.5 0.6 %collective-permute-done.6.refs_5_ = bf16[256,128]{1,0:T(8,128)(2,1)S(1)} collective-permute-done((bf16[256,128]{1,0:T(8,128)(2,1)S(1)}, bf16[256,128]{1,0:T(8,128)(2,1)S(1)}, u32[]{:S(2)}, u32[]{:S(2)}) %collective-permute-start.6) | collective-permute-done | bytes 65568 | tf_op jit(solution)/shard_map/ppermute | solution.py:427
  30.1 0.4 %shard_map.90 = (f32[128,1024]{1,0:T(8,128)S(1)}, bf16[128,256]{1,0:T(8,128)(2,1)S(1)}) custom-call(bf16[8,128,128]{2,1,0:T(8,128)(2,1)S(1)} %get-tuple-element.29.refs_0_, f32[8,128,128]{2,1,0:T(8,128)S(1)} %get-tuple-element.30.refs_4_.refs_1_, bf16[128,1024]{1,0:T(8,128)(2,1)S(1)} %copy-done.1, f32[1,128]{1,0:T(1,128)S(1)} %bitcast.3, ...), custom_call_target="tpu_custom_call" | custom-call | flops 67108864 | bytes 1048576 | tf_op jit(solution)/shard_map/pallas_call | solution.py:499
  30.5 0.9 %collective-permute-done.7.refs_5_ = bf16[256,128]{1,0:T(8,128)(2,1)S(1)} collective-permute-done((bf16[256,128]{1,0:T(8,128)(2,1)S(1)}, bf16[256,128]{1,0:T(8,128)(2,1)S(1)}, u32[]{:S(2)}, u32[]{:S(2)}) %collective-permute-start.7) | collective-permute-done | bytes 65568 | tf_op jit(solution)/shard_map/ppermute | solution.py:427
  31.4 0.4 %shard_map.91 = (bf16[128,1024]{1,0:T(8,128)(2,1)S(1)}, bf16[128,256]{1,0:T(8,128)(2,1)S(1)}) custom-call(bf16[8,128,128]{2,1,0:T(8,128)(2,1)S(1)} %get-tuple-element.29.refs_0_, f32[8,128,128]{2,1,0:T(8,128)S(1)} %get-tuple-element.30.refs_4_.refs_1_, bf16[128,1024]{1,0:T(8,128)(2,1)S(1)} %copy-done.1, f32[1,128]{1,0:T(1,128)S(1)} %bitcast.4, ...), custom_call_target="tpu_custom_call" | custom-call | flops 67108864 | bytes 1048576 | tf_op jit(solution)/shard_map/pallas_call | solution.py:499
  31.9 0.1 collective-permute-start.8
  31.9 0.5 %shard_map.92 = f32[128,1024]{1,0:T(8,128)S(1)} custom-call(bf16[1024,2048]{1,0:T(8,128)(2,1)S(1)} %copy-done, bf16[128,256]{1,0:T(8,128)(2,1)S(1)} %get-tuple-element.42.refs_1_, bf16[128,256]{1,0:T(8,128)(2,1)S(1)} %get-tuple-element.45.refs_2_, bf16[128,256]{1,0:T(8,128)(2,1)S(1)} %get-tuple-element.48.refs_3_, bf16[128,256]{1,0:T(8,128)(2,1)S(1)} %get-tuple-element.51.refs_4_), custom_call_target="tpu_custom_call" | custom-call | flops 268435456 | bytes 1048576 | tf_op jit(solution)/shard_map/pallas_call | solution.py:509
  32.4 1.0 %collective-permute-done.8 = bf16[128,1024]{1,0:T(8,128)(2,1)S(1)} collective-permute-done((bf16[128,1024]{1,0:T(8,128)(2,1)S(1)}, bf16[128,1024]{1,0:T(8,128)(2,1)S(1)}, u32[]{:S(2)}, u32[]{:S(2)}) %collective-permute-start.8) | collective-permute-done | bytes 262176 | tf_op jit(solution)/shard_map/ppermute | solution.py:508
  33.5 0.8 %add_convert_fusion = bf16[128,1024]{1,0:T(8,128)(2,1)} fusion(f32[128,1024]{1,0:T(8,128)S(1)} %shard_map.92, bf16[128,1024]{1,0:T(8,128)(2,1)S(1)} %collective-permute-done.8), kind=kLoop, calls=%fused_computation | loop fusion | flops 393216 | bytes 1048576 | tf_op jit(solution)/shard_map/convert_element_type | solution.py:512
Async XLA Ops:
  1.1 8.4 %collective-permute-start = (bf16[400,128]{1,0:T(8,128)(2,1)S(1)}, bf16[400,128]{1,0:T(8,128)(2,1)S(1)}, u32[]{:S(2)}, u32[]{:S(2)}) collective-permute-start(bf16[400,128]{1,0:T(8,128)(2,1)S(1)} %get-tuple-element.32), channel_id=1, source_target_pairs={{0,6},{1,7},{2,4},{3,5},{4,2},{5,3},{6,0},{7,1},{8,14},{9,15},{10,... | collective-permute-start | bytes 307208 | tf_op jit(solution)/shard_map/ppermute | solution.py:427
  5.1 5.4 %collective-permute-start.1 = (bf16[400,128]{1,0:T(8,128)(2,1)S(1)}, bf16[400,128]{1,0:T(8,128)(2,1)S(1)}, u32[]{:S(2)}, u32[]{:S(2)}) collective-permute-start(bf16[400,128]{1,0:T(8,128)(2,1)S(1)} %get-tuple-element.33), channel_id=1, source_target_pairs={{0,2},{1,5},{2,0},{3,7},{4,6},{5,1},{6,4},{7,3},{8,10},{9,13},{10,... | collective-permute-start | bytes 307208 | tf_op jit(solution)/shard_map/ppermute | solution.py:427
  5.6 21.7 %copy-start = (bf16[1024,2048]{1,0:T(8,128)(2,1)S(1)}, bf16[1024,2048]{1,0:T(8,128)(2,1)}, u32[]{:S(2)}) copy-start(bf16[1024,2048]{1,0:T(8,128)(2,1)} %refs_0_.5) | copy-start | bytes 12582916
  5.6 21.7 %copy-start.1 = (bf16[128,1024]{1,0:T(8,128)(2,1)S(1)}, bf16[128,1024]{1,0:T(8,128)(2,1)}, u32[]{:S(2)}) copy-start(bf16[128,1024]{1,0:T(8,128)(2,1)} %refs_2_.11) | copy-start | bytes 786436
  5.6 21.7 %copy-start.2 = (f32[128]{0:T(128)S(1)}, f32[128]{0:T(128)}, u32[]{:S(2)}) copy-start(f32[128]{0:T(128)} %param.14) | copy-start | bytes 1540
  5.6 4.8 %collective-permute-start.2 = (bf16[400,128]{1,0:T(8,128)(2,1)S(1)}, bf16[400,128]{1,0:T(8,128)(2,1)S(1)}, u32[]{:S(2)}, u32[]{:S(2)}) collective-permute-start(bf16[400,128]{1,0:T(8,128)(2,1)S(1)} %get-tuple-element.34), channel_id=1, source_target_pairs={{0,4},{1,3},{2,6},{3,1},{4,0},{5,7},{6,2},{7,5},{8,12},{9,11},{10,... | collective-permute-start | bytes 307208 | tf_op jit(solution)/shard_map/ppermute | solution.py:427
  13.0 5.1 %collective-permute-start.3 = (bf16[272,256]{1,0:T(8,128)(2,1)S(1)}, bf16[272,256]{1,0:T(8,128)(2,1)S(1)}, u32[]{:S(2)}, u32[]{:S(2)}) collective-permute-start(bf16[272,256]{1,0:T(8,128)(2,1)S(1)} %get-tuple-element.38.refs_0_), channel_id=1, source_target_pairs={{0,8},{2,10},{4,12},{6,14},{8,0},{10,2},{12,4},{14,6},{16,24},{18,... | collective-permute-start | bytes 417800 | tf_op jit(solution)/shard_map/ppermute | solution.py:421
  18.3 5.2 %collective-permute-start.4 = (bf16[256,128]{1,0:T(8,128)(2,1)S(1)}, bf16[256,128]{1,0:T(8,128)(2,1)S(1)}, u32[]{:S(2)}, u32[]{:S(2)}) collective-permute-start(bf16[256,128]{1,0:T(8,128)(2,1)S(1)} %shard_map.86), channel_id=1, source_target_pairs={{0,16},{2,18},{4,20},{6,22},{8,24},{10,26},{12,28},{14,30},{16,0},... | collective-permute-start | bytes 196616 | tf_op jit(solution)/shard_map/ppermute | solution.py:421
  23.8 5.2 %collective-permute-start.5 = (bf16[256,128]{1,0:T(8,128)(2,1)S(1)}, bf16[256,128]{1,0:T(8,128)(2,1)S(1)}, u32[]{:S(2)}, u32[]{:S(2)}) collective-permute-start(bf16[256,128]{1,0:T(8,128)(2,1)S(1)} %get-tuple-element.43), channel_id=1, source_target_pairs={{0,6},{1,7},{2,4},{3,5},{4,2},{5,3},{6,0},{7,1},{8,14},{9,15},{10,... | collective-permute-start | bytes 196616 | tf_op jit(solution)/shard_map/ppermute | solution.py:427
  25.7 4.4 %collective-permute-start.6 = (bf16[256,128]{1,0:T(8,128)(2,1)S(1)}, bf16[256,128]{1,0:T(8,128)(2,1)S(1)}, u32[]{:S(2)}, u32[]{:S(2)}) collective-permute-start(bf16[256,128]{1,0:T(8,128)(2,1)S(1)} %get-tuple-element.46), channel_id=1, source_target_pairs={{0,2},{1,5},{2,0},{3,7},{4,6},{5,1},{6,4},{7,3},{8,10},{9,13},{10,... | collective-permute-start | bytes 196616 | tf_op jit(solution)/shard_map/ppermute | solution.py:427
  27.2 4.3 %collective-permute-start.7 = (bf16[256,128]{1,0:T(8,128)(2,1)S(1)}, bf16[256,128]{1,0:T(8,128)(2,1)S(1)}, u32[]{:S(2)}, u32[]{:S(2)}) collective-permute-start(bf16[256,128]{1,0:T(8,128)(2,1)S(1)} %get-tuple-element.49), channel_id=1, source_target_pairs={{0,4},{1,3},{2,6},{3,1},{4,0},{5,7},{6,2},{7,5},{8,12},{9,11},{10,... | collective-permute-start | bytes 196616 | tf_op jit(solution)/shard_map/ppermute | solution.py:427
  31.9 1.6 %collective-permute-start.8 = (bf16[128,1024]{1,0:T(8,128)(2,1)S(1)}, bf16[128,1024]{1,0:T(8,128)(2,1)S(1)}, u32[]{:S(2)}, u32[]{:S(2)}) collective-permute-start(bf16[128,1024]{1,0:T(8,128)(2,1)S(1)} %get-tuple-element.52), channel_id=1, source_target_pairs={{0,1},{1,0},{2,3},{3,2},{4,5},{5,4},{6,7},{7,6},{8,9},{9,8},{10,11... | collective-permute-start | bytes 786440 | tf_op jit(solution)/shard_map/ppermute | solution.py:508
where the time goes:
time: 34.4 us; the launch traced here: 34.2 us
  starting transfers between devices  12.5 us (36%)
  Pallas kernels  10.6 us (31%)
  waiting for transfers between devices  10.2 us (30%)
  other arithmetic  0.76 us (2%)
    ppermute x6, starting transfers between devices, swap_slots(): came.append(lax.ppermute(x, ('seq', 'head'), pairs))  8.16 us
    ppermute x2, waiting for transfers between devices, swap(): return lax.ppermute(x, 'seq', [(i, i ^ flip) for i in range(ranks)])  5.5 us
    ppermute x2, starting transfers between devices, swap(): return lax.ppermute(x, 'seq', [(i, i ^ flip) for i in range(ranks)])  4.3 us
    pallas_call x1, Pallas kernels, per_device(): call(placed(functools.partial(terms_body, dk, dv, rep, group), group), [s...  3.8 us
    ppermute x6, waiting for transfers between devices, swap_slots(): came.append(lax.ppermute(x, ('seq', 'head'), pairs))  3.67 us
    pallas_call x1, Pallas kernels, per_device(): call(placed(functools.partial(owner_body, dk, dv, rep, group, steps > 1),...  2.59 us
    pallas_call x4, Pallas kernels, per_device(): call(placed(functools.partial(project_body, dk, dv, rep, group, n), group...  1.71 us
    pallas_call x1, Pallas kernels, per_device(): call(placed(functools.partial(pack_body, dk, dv, rep, group), group), [pa...  1.09 us
  transfers between devices with their start and end apart: 9, of which 7 were waited for; matrix products, arithmetic and copies ran while one was open for 0% of the time, Pallas kernels for 18%

commit v1 on v0

--- a/solution.py
+++ b/solution.py
@@ -10,7 +10,7 @@
 F32 = jnp.float32
 BF16 = jnp.bfloat16
 EPS = 1e-06
-LEAF = 32
+LEAF = 16
 PAD = 16
 SMALL = pltpu.CompilerParams(vmem_limit_bytes=24 * 1024 * 1024)
 
@@ -420,11 +420,12 @@
     def swap(x, flip):
         return lax.ppermute(x, "seq", [(i, i ^ flip) for i in range(ranks)])
 
-    def swap_slots(made):
-        came = [made[0]]
-        for x, *flip in list(zip(made, *tours(group)))[1:]:
+    def swap_slots(made, order):
+        came = [made[0]] + [None] * (group - 1)
+        for n in order:
+            x, flip = made[n], [tour[n] for tour in tours(group)]
             pairs = [(i * halves + c, (i ^ flip[c]) * halves + c) for i in range(ranks) for c in (0, 1)]
-            came.append(lax.ppermute(x, ("seq", "head"), pairs))
+            came[n] = lax.ppermute(x, ("seq", "head"), pairs)
         return came
 
     q_in, k_in, v_in, rate_in, decay_in = [
@@ -439,7 +440,7 @@
         [hbm] * 4,
         small + [pltpu.SemaphoreType.DMA((2 + (rep + 1) * group,))],
     )(k_in, v_in, rate_in, decay_in)
-    packs = swap_slots(packs)
+    packs = swap_slots(packs, range(1, group))
     x, y = call(
         placed(functools.partial(terms_body, dk, dv, rep, group), group),
         [shape((heads, tokens, dk), BF16), shape((heads, tokens, dv), F32)],
@@ -490,12 +491,13 @@
         (),
         cube * jobs,
     )(a, b, feed)
-    states = swap_slots(states)
+    last = list(range(1, group))[::-1]
+    states = swap_slots(states, last)
 
     work = 2 * tokens * columns * heads * dv
-    away, normed = [], []
-    for n, state in enumerate(states):
-        kind = F32 if n < group - 1 else BF16
+    away, normed = [], [None] * group
+    for n in [0] + last:
+        state, kind = states[n], F32 if n != last[-1] else BF16
         total, piece = call(
             placed(functools.partial(project_body, dk, dv, rep, group, n), group),
             [shape((tokens, columns), kind), shape((tokens, rep * dv), BF16)],
@@ -504,7 +506,7 @@
             work // group,
         )(x, y, out_gate, norm_gain.reshape(1, dv), out_weight, state, *away)
         away = [total]
-        normed.append(piece)
+        normed[n] = piece
     came = lax.ppermute(away[0], "head", [(0, 1), (1, 0)])
     own = call(placed(functools.partial(own_body, group), group), shape((tokens, columns), F32), [vmem] * (1 + group), (), work)(
         out_weight, *normed

time: 34.4 us -> 34.4 us (level)
  no operation moved by 1% of the time
where the time goes in v1:
time: 34.4 us; the launch traced here: 34.3 us
  starting transfers between devices  12.5 us (36%)
  Pallas kernels  10.7 us (31%)
  waiting for transfers between devices  10.1 us (29%)
  other arithmetic  0.76 us (2%)
    ppermute x6, starting transfers between devices, swap_slots(): came[n] = lax.ppermute(x, ('seq', 'head'), pairs)  8.15 us
    ppermute x2, waiting for transfers between devices, swap(): return lax.ppermute(x, 'seq', [(i, i ^ flip) for i in range(ranks)])  5.5 us
    ppermute x2, starting transfers between devices, swap(): return lax.ppermute(x, 'seq', [(i, i ^ flip) for i in range(ranks)])  4.3 us
    pallas_call x1, Pallas kernels, per_device(): call(placed(functools.partial(terms_body, dk, dv, rep, group), group), [s...  3.85 us
    ppermute x6, waiting for transfers between devices, swap_slots(): came[n] = lax.ppermute(x, ('seq', 'head'), pairs)  3.63 us
    pallas_call x1, Pallas kernels, per_device(): call(placed(functools.partial(owner_body, dk, dv, rep, group, steps > 1),...  2.61 us
    pallas_call x4, Pallas kernels, per_device(): call(placed(functools.partial(project_body, dk, dv, rep, group, n), group...  1.71 us
    pallas_call x1, Pallas kernels, per_device(): call(placed(functools.partial(pack_body, dk, dv, rep, group), group), [pa...  1.09 us
  transfers between devices with their start and end apart: 9, of which 7 were waited for; matrix products, arithmetic and copies ran while one was open for 0% of the time, Pallas kernels for 18%

profile of v1, /device:TPU:0, one launch (start us, length us, event | category | flops | bytes accessed | tf_op | source)
XLA Modules:
  0.0 34.3 jit_solution(11044798174638031820)
XLA Ops:
  0.0 1.1 %shard_map.83 = (bf16[400,128]{1,0:T(8,128)(2,1)S(1)}, bf16[400,128]{1,0:T(8,128)(2,1)S(1)}, bf16[400,128]{1,0:T(8,128)(2,1)S(1)}, bf16[400,128]{1,0:T(8,128)(2,1)S(1)}) custom-call(bf16[128,512]{1,0:T(8,128)(2,1)} %refs_0_.4, bf16[128,1024]{1,0:T(8,128)(2,1)} %refs_1_.3, f32[8,128]{1,0:T(8,128)} %refs_2_.7, f32[8,128]{1,0:T(8,128)} %refs_3_.3), custom_call_target="tpu_custom_call" | custom-call | bytes 1048576 | tf_op jit(solution)/shard_map/pallas_call | solution.py:437
  1.1 4.0 %collective-permute-start = (bf16[400,128]{1,0:T(8,128)(2,1)S(1)}, bf16[400,128]{1,0:T(8,128)(2,1)S(1)}, u32[]{:S(2)}, u32[]{:S(2)}) collective-permute-start(bf16[400,128]{1,0:T(8,128)(2,1)S(1)} %get-tuple-element.32), channel_id=1, source_target_pairs={{0,6},{1,7},{2,4},{3,5},{4,2},{5,3},{6,0},{7,1},{8,14},{9,15},{10,... | collective-permute-start | bytes 307208 | tf_op jit(solution)/shard_map/ppermute | solution.py:428
  5.1 0.5 %collective-permute-start.1 = (bf16[400,128]{1,0:T(8,128)(2,1)S(1)}, bf16[400,128]{1,0:T(8,128)(2,1)S(1)}, u32[]{:S(2)}, u32[]{:S(2)}) collective-permute-start(bf16[400,128]{1,0:T(8,128)(2,1)S(1)} %get-tuple-element.33), channel_id=1, source_target_pairs={{0,2},{1,5},{2,0},{3,7},{4,6},{5,1},{6,4},{7,3},{8,10},{9,13},{10,... | collective-permute-start | bytes 307208 | tf_op jit(solution)/shard_map/ppermute | solution.py:428
  5.6 0.0 copy-start
  5.6 0.0 copy-start.1
  5.6 0.0 copy-start.2
  5.6 0.1 collective-permute-start.2
  5.7 3.8 %shard_map.82 = (bf16[8,128,128]{2,1,0:T(8,128)(2,1)S(1)}, f32[8,128,128]{2,1,0:T(8,128)S(1)}) custom-call(bf16[128,512]{1,0:T(8,128)(2,1)} %refs_0_.3, bf16[128,512]{1,0:T(8,128)(2,1)} %refs_0_.4, bf16[128,1024]{1,0:T(8,128)(2,1)} %refs_1_.3, f32[8,128]{1,0:T(8,128)} %refs_2_.7, f32[8,128]{1,0:T(8,128)} %refs_3_.3), custom_call_target="tpu_custom_call" | custom-call | flops 1073741824 | bytes 1048576 | tf_op jit(solution)/shard_map/pallas_call | solution.py:444
  9.6 0.0 collective-permute-done.refs_1_
  9.6 0.8 %collective-permute-done.1.refs_2_ = bf16[400,128]{1,0:T(8,128)(2,1)S(1)} collective-permute-done((bf16[400,128]{1,0:T(8,128)(2,1)S(1)}, bf16[400,128]{1,0:T(8,128)(2,1)S(1)}, u32[]{:S(2)}, u32[]{:S(2)}) %collective-permute-start.1) | collective-permute-done | bytes 102432 | tf_op jit(solution)/shard_map/ppermute | solution.py:428
  10.4 0.0 collective-permute-done.2.refs_3_
  10.4 2.6 %shard_map.84 = (bf16[272,256]{1,0:T(8,128)(2,1)S(1)}, bf16[8,128,128]{2,1,0:T(8,128)(2,1)S(1)}, f32[8,128,128]{2,1,0:T(8,128)S(1)}, f32[8,128]{1,0:T(8,128)S(1)}) custom-call(bf16[400,128]{1,0:T(8,128)(2,1)S(1)} %get-tuple-element.31.refs_0_, bf16[400,128]{1,0:T(8,128)(2,1)S(1)} %collective-permute-done.refs_1_, ...), custom_call_target="tpu_custom_call" | custom-call | flops 1073741824 | bytes 1048576 | tf_op jit(solution)/shard_map/pallas_call | solution.py:454
  13.0 1.6 %collective-permute-start.3 = (bf16[272,256]{1,0:T(8,128)(2,1)S(1)}, bf16[272,256]{1,0:T(8,128)(2,1)S(1)}, u32[]{:S(2)}, u32[]{:S(2)}) collective-permute-start(bf16[272,256]{1,0:T(8,128)(2,1)S(1)} %get-tuple-element.38.refs_0_), channel_id=1, source_target_pairs={{0,8},{2,10},{4,12},{6,14},{8,0},{10,2},{12,4},{14,6},{16,24},{18,... | collective-permute-start | bytes 417800 | tf_op jit(solution)/shard_map/ppermute | solution.py:421
  14.7 3.5 %collective-permute-done.3.refs_3_.refs_1_ = bf16[272,256]{1,0:T(8,128)(2,1)S(1)} collective-permute-done((bf16[272,256]{1,0:T(8,128)(2,1)S(1)}, bf16[272,256]{1,0:T(8,128)(2,1)S(1)}, u32[]{:S(2)}, u32[]{:S(2)}) %collective-permute-start.3) | collective-permute-done | bytes 139296 | tf_op jit(solution)/shard_map/ppermute | solution.py:421
  18.2 0.2 shard_map.86
  18.4 2.7 %collective-permute-start.4 = (bf16[256,128]{1,0:T(8,128)(2,1)S(1)}, bf16[256,128]{1,0:T(8,128)(2,1)S(1)}, u32[]{:S(2)}, u32[]{:S(2)}) collective-permute-start(bf16[256,128]{1,0:T(8,128)(2,1)S(1)} %shard_map.86), channel_id=1, source_target_pairs={{0,16},{2,18},{4,20},{6,22},{8,24},{10,26},{12,28},{14,30},{16,0},... | collective-permute-start | bytes 196616 | tf_op jit(solution)/shard_map/ppermute | solution.py:421
  21.0 0.5 %shard_map.85 = (bf16[4,2,128,128]{3,2,1,0:T(8,128)(2,1)S(1)}, f32[4,2,128,128]{3,2,1,0:T(8,128)S(1)}) custom-call(bf16[8,128,128]{2,1,0:T(8,128)(2,1)S(1)} %get-tuple-element.35.refs_0_, f32[8,128,128]{2,1,0:T(8,128)S(1)} %get-tuple-element.36.refs_1_, f32[8,128]{1,0:T(8,128)S(1)} %get-tuple-element.37.refs_2_, ...), custom_call_target="tpu_custom_call" | custom-call | flops 268435456 | bytes 1048576 | tf_op jit(solution)/shard_map/pallas_call | solution.py:480
  21.6 2.0 %collective-permute-done.4.refs_2_ = bf16[256,128]{1,0:T(8,128)(2,1)S(1)} collective-permute-done((bf16[256,128]{1,0:T(8,128)(2,1)S(1)}, bf16[256,128]{1,0:T(8,128)(2,1)S(1)}, u32[]{:S(2)}, u32[]{:S(2)}) %collective-permute-start.4) | collective-permute-done | bytes 65568 | tf_op jit(solution)/shard_map/ppermute | solution.py:421
  23.6 0.2 shard_map.87
  23.8 1.9 %collective-permute-start.7 = (bf16[256,128]{1,0:T(8,128)(2,1)S(1)}, bf16[256,128]{1,0:T(8,128)(2,1)S(1)}, u32[]{:S(2)}, u32[]{:S(2)}) collective-permute-start(bf16[256,128]{1,0:T(8,128)(2,1)S(1)} %get-tuple-element.45), channel_id=1, source_target_pairs={{0,4},{1,3},{2,6},{3,1},{4,0},{5,7},{6,2},{7,5},{8,12},{9,11},{10,... | collective-permute-start | bytes 196616 | tf_op jit(solution)/shard_map/ppermute | solution.py:428
  25.7 0.6 %collective-permute-start.6 = (bf16[256,128]{1,0:T(8,128)(2,1)S(1)}, bf16[256,128]{1,0:T(8,128)(2,1)S(1)}, u32[]{:S(2)}, u32[]{:S(2)}) collective-permute-start(bf16[256,128]{1,0:T(8,128)(2,1)S(1)} %get-tuple-element.44), channel_id=1, source_target_pairs={{0,2},{1,5},{2,0},{3,7},{4,6},{5,1},{6,4},{7,3},{8,10},{9,13},{10,... | collective-permute-start | bytes 196616 | tf_op jit(solution)/shard_map/ppermute | solution.py:428
  26.3 1.1 %collective-permute-start.5 = (bf16[256,128]{1,0:T(8,128)(2,1)S(1)}, bf16[256,128]{1,0:T(8,128)(2,1)S(1)}, u32[]{:S(2)}, u32[]{:S(2)}) collective-permute-start(bf16[256,128]{1,0:T(8,128)(2,1)S(1)} %get-tuple-element.43), channel_id=1, source_target_pairs={{0,6},{1,7},{2,4},{3,5},{4,2},{5,3},{6,0},{7,1},{8,14},{9,15},{10,... | collective-permute-start | bytes 196616 | tf_op jit(solution)/shard_map/ppermute | solution.py:428
  27.4 0.0 copy-done
  27.4 0.0 copy-done.1
  27.4 0.0 copy-done.2
  27.4 0.4 %shard_map.88 = (f32[128,1024]{1,0:T(8,128)S(1)}, bf16[128,256]{1,0:T(8,128)(2,1)S(1)}) custom-call(bf16[8,128,128]{2,1,0:T(8,128)(2,1)S(1)} %get-tuple-element.29.refs_0_, f32[8,128,128]{2,1,0:T(8,128)S(1)} %get-tuple-element.30.refs_4_.refs_1_, bf16[128,1024]{1,0:T(8,128)(2,1)S(1)} %copy-done.1, f32[1,128]{1,0:T(1,128)S(1)} %bitcast.1, ...), custom_call_target="tpu_custom_call" | custom-call | flops 67108864 | bytes 1048576 | tf_op jit(solution)/shard_map/pallas_call | solution.py:501
  27.8 1.0 %collective-permute-done.7.refs_5_ = bf16[256,128]{1,0:T(8,128)(2,1)S(1)} collective-permute-done((bf16[256,128]{1,0:T(8,128)(2,1)S(1)}, bf16[256,128]{1,0:T(8,128)(2,1)S(1)}, u32[]{:S(2)}, u32[]{:S(2)}) %collective-permute-start.7) | collective-permute-done | bytes 65568 | tf_op jit(solution)/shard_map/ppermute | solution.py:428
  28.8 0.4 %shard_map.89 = (f32[128,1024]{1,0:T(8,128)S(1)}, bf16[128,256]{1,0:T(8,128)(2,1)S(1)}) custom-call(bf16[8,128,128]{2,1,0:T(8,128)(2,1)S(1)} %get-tuple-element.29.refs_0_, f32[8,128,128]{2,1,0:T(8,128)S(1)} %get-tuple-element.30.refs_4_.refs_1_, bf16[128,1024]{1,0:T(8,128)(2,1)S(1)} %copy-done.1, f32[1,128]{1,0:T(1,128)S(1)} %bitcast.2, ...), custom_call_target="tpu_custom_call" | custom-call | flops 67108864 | bytes 1048576 | tf_op jit(solution)/shard_map/pallas_call | solution.py:501
  29.3 0.7 %collective-permute-done.6.refs_5_ = bf16[256,128]{1,0:T(8,128)(2,1)S(1)} collective-permute-done((bf16[256,128]{1,0:T(8,128)(2,1)S(1)}, bf16[256,128]{1,0:T(8,128)(2,1)S(1)}, u32[]{:S(2)}, u32[]{:S(2)}) %collective-permute-start.6) | collective-permute-done | bytes 65568 | tf_op jit(solution)/shard_map/ppermute | solution.py:428
  30.0 0.4 %shard_map.90 = (f32[128,1024]{1,0:T(8,128)S(1)}, bf16[128,256]{1,0:T(8,128)(2,1)S(1)}) custom-call(bf16[8,128,128]{2,1,0:T(8,128)(2,1)S(1)} %get-tuple-element.29.refs_0_, f32[8,128,128]{2,1,0:T(8,128)S(1)} %get-tuple-element.30.refs_4_.refs_1_, bf16[128,1024]{1,0:T(8,128)(2,1)S(1)} %copy-done.1, f32[1,128]{1,0:T(1,128)S(1)} %bitcast.3, ...), custom_call_target="tpu_custom_call" | custom-call | flops 67108864 | bytes 1048576 | tf_op jit(solution)/shard_map/pallas_call | solution.py:501
  30.4 1.1 %collective-permute-done.5.refs_5_ = bf16[256,128]{1,0:T(8,128)(2,1)S(1)} collective-permute-done((bf16[256,128]{1,0:T(8,128)(2,1)S(1)}, bf16[256,128]{1,0:T(8,128)(2,1)S(1)}, u32[]{:S(2)}, u32[]{:S(2)}) %collective-permute-start.5) | collective-permute-done | bytes 65568 | tf_op jit(solution)/shard_map/ppermute | solution.py:428
  31.5 0.4 %shard_map.91 = (bf16[128,1024]{1,0:T(8,128)(2,1)S(1)}, bf16[128,256]{1,0:T(8,128)(2,1)S(1)}) custom-call(bf16[8,128,128]{2,1,0:T(8,128)(2,1)S(1)} %get-tuple-element.29.refs_0_, f32[8,128,128]{2,1,0:T(8,128)S(1)} %get-tuple-element.30.refs_4_.refs_1_, bf16[128,1024]{1,0:T(8,128)(2,1)S(1)} %copy-done.1, f32[1,128]{1,0:T(1,128)S(1)} %bitcast.4, ...), custom_call_target="tpu_custom_call" | custom-call | flops 67108864 | bytes 1048576 | tf_op jit(solution)/shard_map/pallas_call | solution.py:501
  31.9 0.1 collective-permute-start.8
  32.0 0.5 %shard_map.92 = f32[128,1024]{1,0:T(8,128)S(1)} custom-call(bf16[1024,2048]{1,0:T(8,128)(2,1)S(1)} %copy-done, bf16[128,256]{1,0:T(8,128)(2,1)S(1)} %get-tuple-element.42.refs_1_, bf16[128,256]{1,0:T(8,128)(2,1)S(1)} %get-tuple-element.49.refs_2_, bf16[128,256]{1,0:T(8,128)(2,1)S(1)} %get-tuple-element.50.refs_3_, bf16[128,256]{1,0:T(8,128)(2,1)S(1)} %get-tuple-element.51.refs_4_), custom_call_target="tpu_custom_call" | custom-call | flops 268435456 | bytes 1048576 | tf_op jit(solution)/shard_map/pallas_call | solution.py:511
  32.5 1.0 %collective-permute-done.8 = bf16[128,1024]{1,0:T(8,128)(2,1)S(1)} collective-permute-done((bf16[128,1024]{1,0:T(8,128)(2,1)S(1)}, bf16[128,1024]{1,0:T(8,128)(2,1)S(1)}, u32[]{:S(2)}, u32[]{:S(2)}) %collective-permute-start.8) | collective-permute-done | bytes 262176 | tf_op jit(solution)/shard_map/ppermute | solution.py:510
  33.5 0.8 %add_convert_fusion = bf16[128,1024]{1,0:T(8,128)(2,1)} fusion(f32[128,1024]{1,0:T(8,128)S(1)} %shard_map.92, bf16[128,1024]{1,0:T(8,128)(2,1)S(1)} %collective-permute-done.8), kind=kLoop, calls=%fused_computation | loop fusion | flops 393216 | bytes 1048576 | tf_op jit(solution)/shard_map/convert_element_type | solution.py:514
Async XLA Ops:
  1.1 8.5 %collective-permute-start = (bf16[400,128]{1,0:T(8,128)(2,1)S(1)}, bf16[400,128]{1,0:T(8,128)(2,1)S(1)}, u32[]{:S(2)}, u32[]{:S(2)}) collective-permute-start(bf16[400,128]{1,0:T(8,128)(2,1)S(1)} %get-tuple-element.32), channel_id=1, source_target_pairs={{0,6},{1,7},{2,4},{3,5},{4,2},{5,3},{6,0},{7,1},{8,14},{9,15},{10,... | collective-permute-start | bytes 307208 | tf_op jit(solution)/shard_map/ppermute | solution.py:428
  5.1 5.4 %collective-permute-start.1 = (bf16[400,128]{1,0:T(8,128)(2,1)S(1)}, bf16[400,128]{1,0:T(8,128)(2,1)S(1)}, u32[]{:S(2)}, u32[]{:S(2)}) collective-permute-start(bf16[400,128]{1,0:T(8,128)(2,1)S(1)} %get-tuple-element.33), channel_id=1, source_target_pairs={{0,2},{1,5},{2,0},{3,7},{4,6},{5,1},{6,4},{7,3},{8,10},{9,13},{10,... | collective-permute-start | bytes 307208 | tf_op jit(solution)/shard_map/ppermute | solution.py:428
  5.6 21.8 %copy-start = (bf16[1024,2048]{1,0:T(8,128)(2,1)S(1)}, bf16[1024,2048]{1,0:T(8,128)(2,1)}, u32[]{:S(2)}) copy-start(bf16[1024,2048]{1,0:T(8,128)(2,1)} %refs_0_.5) | copy-start | bytes 12582916
  5.6 21.8 %copy-start.1 = (bf16[128,1024]{1,0:T(8,128)(2,1)S(1)}, bf16[128,1024]{1,0:T(8,128)(2,1)}, u32[]{:S(2)}) copy-start(bf16[128,1024]{1,0:T(8,128)(2,1)} %refs_2_.11) | copy-start | bytes 786436
  5.6 21.8 %copy-start.2 = (f32[128]{0:T(128)S(1)}, f32[128]{0:T(128)}, u32[]{:S(2)}) copy-start(f32[128]{0:T(128)} %param.14) | copy-start | bytes 1540
  5.6 4.8 %collective-permute-start.2 = (bf16[400,128]{1,0:T(8,128)(2,1)S(1)}, bf16[400,128]{1,0:T(8,128)(2,1)S(1)}, u32[]{:S(2)}, u32[]{:S(2)}) collective-permute-start(bf16[400,128]{1,0:T(8,128)(2,1)S(1)} %get-tuple-element.34), channel_id=1, source_target_pairs={{0,4},{1,3},{2,6},{3,1},{4,0},{5,7},{6,2},{7,5},{8,12},{9,11},{10,... | collective-permute-start | bytes 307208 | tf_op jit(solution)/shard_map/ppermute | solution.py:428
  13.0 5.1 %collective-permute-start.3 = (bf16[272,256]{1,0:T(8,128)(2,1)S(1)}, bf16[272,256]{1,0:T(8,128)(2,1)S(1)}, u32[]{:S(2)}, u32[]{:S(2)}) collective-permute-start(bf16[272,256]{1,0:T(8,128)(2,1)S(1)} %get-tuple-element.38.refs_0_), channel_id=1, source_target_pairs={{0,8},{2,10},{4,12},{6,14},{8,0},{10,2},{12,4},{14,6},{16,24},{18,... | collective-permute-start | bytes 417800 | tf_op jit(solution)/shard_map/ppermute | solution.py:421
  18.4 5.2 %collective-permute-start.4 = (bf16[256,128]{1,0:T(8,128)(2,1)S(1)}, bf16[256,128]{1,0:T(8,128)(2,1)S(1)}, u32[]{:S(2)}, u32[]{:S(2)}) collective-permute-start(bf16[256,128]{1,0:T(8,128)(2,1)S(1)} %shard_map.86), channel_id=1, source_target_pairs={{0,16},{2,18},{4,20},{6,22},{8,24},{10,26},{12,28},{14,30},{16,0},... | collective-permute-start | bytes 196616 | tf_op jit(solution)/shard_map/ppermute | solution.py:421
  23.8 5.0 %collective-permute-start.7 = (bf16[256,128]{1,0:T(8,128)(2,1)S(1)}, bf16[256,128]{1,0:T(8,128)(2,1)S(1)}, u32[]{:S(2)}, u32[]{:S(2)}) collective-permute-start(bf16[256,128]{1,0:T(8,128)(2,1)S(1)} %get-tuple-element.45), channel_id=1, source_target_pairs={{0,4},{1,3},{2,6},{3,1},{4,0},{5,7},{6,2},{7,5},{8,12},{9,11},{10,... | collective-permute-start | bytes 196616 | tf_op jit(solution)/shard_map/ppermute | solution.py:428
  25.7 4.3 %collective-permute-start.6 = (bf16[256,128]{1,0:T(8,128)(2,1)S(1)}, bf16[256,128]{1,0:T(8,128)(2,1)S(1)}, u32[]{:S(2)}, u32[]{:S(2)}) collective-permute-start(bf16[256,128]{1,0:T(8,128)(2,1)S(1)} %get-tuple-element.44), channel_id=1, source_target_pairs={{0,2},{1,5},{2,0},{3,7},{4,6},{5,1},{6,4},{7,3},{8,10},{9,13},{10,... | collective-permute-start | bytes 196616 | tf_op jit(solution)/shard_map/ppermute | solution.py:428
  26.3 5.2 %collective-permute-start.5 = (bf16[256,128]{1,0:T(8,128)(2,1)S(1)}, bf16[256,128]{1,0:T(8,128)(2,1)S(1)}, u32[]{:S(2)}, u32[]{:S(2)}) collective-permute-start(bf16[256,128]{1,0:T(8,128)(2,1)S(1)} %get-tuple-element.43), channel_id=1, source_target_pairs={{0,6},{1,7},{2,4},{3,5},{4,2},{5,3},{6,0},{7,1},{8,14},{9,15},{10,... | collective-permute-start | bytes 196616 | tf_op jit(solution)/shard_map/ppermute | solution.py:428
  31.9 1.6 %collective-permute-start.8 = (bf16[128,1024]{1,0:T(8,128)(2,1)S(1)}, bf16[128,1024]{1,0:T(8,128)(2,1)S(1)}, u32[]{:S(2)}, u32[]{:S(2)}) collective-permute-start(bf16[128,1024]{1,0:T(8,128)(2,1)S(1)} %get-tuple-element.52), channel_id=1, source_target_pairs={{0,1},{1,0},{2,3},{3,2},{4,5},{5,4},{6,7},{7,6},{8,9},{9,8},{10,11... | collective-permute-start | bytes 786440 | tf_op jit(solution)/shard_map/ppermute | solution.py:510

commit v2 on v1

--- a/solution.py
+++ b/solution.py
@@ -239,9 +239,9 @@
     return [maps[h::rep] for h in range(rep)]
 
 
-def terms_body(dk, dv, rep, group, where, q_in, k_in, v_in, rate_in, decay_in, *refs):
-    slots = flips(group, where[1])
-    x_ref, y_ref, q_ref, k_ref, v_ref, rate_ref, decay_ref, sems = refs
+def terms_body(dk, dv, rep, group, span, where, q_in, k_in, v_in, rate_in, decay_in, *refs):
+    slots = [flips(group, where[1])[n] for n in span]
+    x_ref, y_ref, q_ref, k_ref, v_ref, rate_ref, decay_ref, sems = refs[-8:]
     tokens = k_in.shape[0]
     rank = where[0]
     pairs = [(rate_in, rate_ref), (decay_in, decay_ref), (k_in, k_ref), (v_in, v_ref), (q_in, q_ref)]
@@ -308,7 +308,8 @@
         ref[h * feed.shape[0] : (h + 1) * feed.shape[0], :] = feed.astype(BF16)
 
 
-def block_body(dk, rep, step, whole, where, own_ref, came_ref, out_ref):
+def block_body(dk, rep, step, whole, where, own_ref, came_ref, *rest):
+    out_ref = rest[-1]
     own, came = load_maps(own_ref, dk, rep), load_maps(came_ref, dk, rep)
     flag = (where[2] >> step) & 1
     late, early = pick(flag, own, came), pick(flag, came, own)
@@ -354,13 +355,13 @@
             out[rows, :] = (dot(a_ref[at, h], feed[rows]) + b_ref[at, h]).astype(BF16)
 
 
-def project_body(dk, dv, rep, group, at, where, x_ref, y_ref, gate_ref, gain_ref, w_ref, state, *refs):
+def project_body(dk, dv, rep, group, at, first, where, x_ref, y_ref, gate_ref, gain_ref, w_ref, state, *refs):
     slots = flips(group, where[1])
     *before, out_ref, normed_ref = refs
     own = (where[0] ^ slots[at]) * rep
     outs = []
     for h in range(rep):
-        n = at * rep + h
+        n = (at - first) * rep + h
         outs.append(dot(x_ref[n], state[h * dk : (h + 1) * dk, :]) + y_ref[n])
     scaled, scales = [], []
     for h, o in enumerate(outs):
@@ -441,15 +442,22 @@
         small + [pltpu.SemaphoreType.DMA((2 + (rep + 1) * group,))],
     )(k_in, v_in, rate_in, decay_in)
     packs = swap_slots(packs, range(1, group))
-    x, y = call(
-        placed(functools.partial(terms_body, dk, dv, rep, group), group),
-        [shape((heads, tokens, dk), BF16), shape((heads, tokens, dv), F32)],
-        [hbm] * 5,
-        [pltpu.VMEM(z.shape, BF16) for z in (queries, key_rows, values)]
-        + small
-        + [pltpu.SemaphoreType.DMA((5,))],
-        heads * 16 * cube,
-    )(q_in, k_in, v_in, rate_in, decay_in)
+    inputs = q_in, k_in, v_in, rate_in, decay_in
+
+    def terms(span, *after):
+        count = len(span) * rep
+        return call(
+            placed(functools.partial(terms_body, dk, dv, rep, group, span), group),
+            [shape((count, tokens, dk), BF16), shape((count, tokens, dv), F32)],
+            [hbm] * 5 + [pl.ANY] * len(after),
+            [pltpu.VMEM(z.shape, BF16) for z in (queries, key_rows, values)]
+            + small
+            + [pltpu.SemaphoreType.DMA((5,))],
+            count * 16 * cube,
+        )(*inputs, *after)
+
+    cut = group // 2
+    xy = [terms(list(range(cut)))]
     jobs = group * rep
     send, *blocks = call(
         placed(functools.partial(owner_body, dk, dv, rep, group, steps > 1), group),
@@ -462,7 +470,8 @@
         [vmem] * group + [pl.ANY],
         [pltpu.VMEM((group,) + pack_shape.shape, BF16)],
         jobs * 16 * cube,
-    )(*packs, y)
+    )(*packs, xy[0][1])
+    xy.append(terms(list(range(cut, group)), send))
 
     came, feed = [], send
     for step in range(steps):
@@ -474,8 +483,8 @@
         send = call(
             placed(functools.partial(block_body, dk, rep, step, whole), group),
             map_shape if whole else feed_shape,
-            [vmem] * 2,
-        )(send, got)
+            [vmem] * 2 + [pl.ANY],
+        )(send, got, xy[1][1])
         came.append(got)
     a, b = call(
         placed(functools.partial(prefix_body, dk, rep), group),
@@ -499,12 +508,12 @@
     for n in [0] + last:
         state, kind = states[n], F32 if n != last[-1] else BF16
         total, piece = call(
-            placed(functools.partial(project_body, dk, dv, rep, group, n), group),
+            placed(functools.partial(project_body, dk, dv, rep, group, n, n // cut * cut), group),
             [shape((tokens, columns), kind), shape((tokens, rep * dv), BF16)],
             [vmem] * (6 + len(away)),
             (),
             work // group,
-        )(x, y, out_gate, norm_gain.reshape(1, dv), out_weight, state, *away)
+        )(*xy[n // cut], out_gate, norm_gain.reshape(1, dv), out_weight, state, *away)
         away = [total]
         normed[n] = piece
     came = lax.ppermute(away[0], "head", [(0, 1), (1, 0)])

time: 34.4 us -> 34.4 us (level)
  Pallas kernels: 10.7 us -> 13.2 us
  waiting for transfers between devices: 10.1 us -> 7.66 us
    ppermute x2, waiting for transfers between devices: 5.5 us -> 2.34 us  [swap(): return lax.ppermute(x, 'seq', [(i, i ^ flip) for i in range(ranks)])]
    pallas_call x5 -> x6, Pallas kernels: 5.56 us -> 8.01 us  [the longest x2 6.3 us: terms(): call(placed(functools.partial(terms_body, dk, dv, rep, group, span), grou...]
    ppermute x6, waiting for transfers between devices: 3.63 us -> 4.31 us  [swap_slots(): came[n] = lax.ppermute(x, ('seq', 'head'), pairs)]
  transfers between devices with their start and end apart: 9 -> 9, of which waited for: 7 -> 7; matrix products, arithmetic and copies ran while one was open for 0% -> 0% of each run, Pallas kernels for 18% -> 25%
where the time goes in v2:
time: 34.4 us; the launch traced here: 34.2 us
  Pallas kernels  13.2 us (38%)
  starting transfers between devices  12.5 us (36%)
  waiting for transfers between devices  7.66 us (22%)
  other arithmetic  0.76 us (2%)
    ppermute x6, starting transfers between devices, swap_slots(): came[n] = lax.ppermute(x, ('seq', 'head'), pairs)  8.15 us
    pallas_call x2, Pallas kernels, terms(): call(placed(functools.partial(terms_body, dk, dv, rep, group, span), grou...  6.3 us
    ppermute x6, waiting for transfers between devices, swap_slots(): came[n] = lax.ppermute(x, ('seq', 'head'), pairs)  4.31 us
    ppermute x2, starting transfers between devices, swap(): return lax.ppermute(x, 'seq', [(i, i ^ flip) for i in range(ranks)])  4.3 us
    pallas_call x1, Pallas kernels, per_device(): call(placed(functools.partial(owner_body, dk, dv, rep, group, steps > 1),...  2.61 us
    ppermute x2, waiting for transfers between devices, swap(): return lax.ppermute(x, 'seq', [(i, i ^ flip) for i in range(ranks)])  2.34 us
    pallas_call x4, Pallas kernels, per_device(): call(placed(functools.partial(project_body, dk, dv, rep, group, n, n // c...  1.71 us
    pallas_call x1, Pallas kernels, per_device(): call(placed(functools.partial(pack_body, dk, dv, rep, group), group), [pa...  1.09 us
  transfers between devices with their start and end apart: 9, of which 7 were waited for; matrix products, arithmetic and copies ran while one was open for 0% of the time, Pallas kernels for 25%

profile of v2, /device:TPU:0, one launch (start us, length us, event | category | flops | bytes accessed | tf_op | source)
XLA Modules:
  0.0 34.2 jit_solution(17327156369449697050)
XLA Ops:
  0.0 1.1 %shard_map.83 = (bf16[400,128]{1,0:T(8,128)(2,1)S(1)}, bf16[400,128]{1,0:T(8,128)(2,1)S(1)}, bf16[400,128]{1,0:T(8,128)(2,1)S(1)}, bf16[400,128]{1,0:T(8,128)(2,1)S(1)}) custom-call(bf16[128,512]{1,0:T(8,128)(2,1)} %refs_1_.5, bf16[128,1024]{1,0:T(8,128)(2,1)} %refs_2_.9, f32[8,128]{1,0:T(8,128)} %refs_3_.5, f32[8,128]{1,0:T(8,128)} %refs_4_.7), custom_call_target="tpu_custom_call" | custom-call | bytes 1048576 | tf_op jit(solution)/shard_map/pallas_call | solution.py:438
  1.1 4.0 %collective-permute-start = (bf16[400,128]{1,0:T(8,128)(2,1)S(1)}, bf16[400,128]{1,0:T(8,128)(2,1)S(1)}, u32[]{:S(2)}, u32[]{:S(2)}) collective-permute-start(bf16[400,128]{1,0:T(8,128)(2,1)S(1)} %get-tuple-element.34), channel_id=1, source_target_pairs={{0,6},{1,7},{2,4},{3,5},{4,2},{5,3},{6,0},{7,1},{8,14},{9,15},{10,... | collective-permute-start | bytes 307208 | tf_op jit(solution)/shard_map/ppermute | solution.py:429
  5.1 0.5 %collective-permute-start.1 = (bf16[400,128]{1,0:T(8,128)(2,1)S(1)}, bf16[400,128]{1,0:T(8,128)(2,1)S(1)}, u32[]{:S(2)}, u32[]{:S(2)}) collective-permute-start(bf16[400,128]{1,0:T(8,128)(2,1)S(1)} %get-tuple-element.35), channel_id=1, source_target_pairs={{0,2},{1,5},{2,0},{3,7},{4,6},{5,1},{6,4},{7,3},{8,10},{9,13},{10,... | collective-permute-start | bytes 307208 | tf_op jit(solution)/shard_map/ppermute | solution.py:429
  5.6 0.1 collective-permute-start.2
  5.7 3.1 %shard_map.82 = (bf16[4,128,128]{2,1,0:T(8,128)(2,1)S(1)}, f32[4,128,128]{2,1,0:T(8,128)S(1)}) custom-call(bf16[128,512]{1,0:T(8,128)(2,1)} %refs_0_.6, bf16[128,512]{1,0:T(8,128)(2,1)} %refs_1_.5, bf16[128,1024]{1,0:T(8,128)(2,1)} %refs_2_.9, f32[8,128]{1,0:T(8,128)} %refs_3_.5, f32[8,128]{1,0:T(8,128)} %refs_4_.7), custom_call_target="tpu_custom_call" | custom-call | flops 536870912 | bytes 1048576 | tf_op jit(solution)/shard_map/pallas_call | solution.py:449
  8.9 0.0 collective-permute-done.refs_1_
  8.9 1.6 %collective-permute-done.1.refs_2_ = bf16[400,128]{1,0:T(8,128)(2,1)S(1)} collective-permute-done((bf16[400,128]{1,0:T(8,128)(2,1)S(1)}, bf16[400,128]{1,0:T(8,128)(2,1)S(1)}, u32[]{:S(2)}, u32[]{:S(2)}) %collective-permute-start.1) | collective-permute-done | bytes 102432 | tf_op jit(solution)/shard_map/ppermute | solution.py:429
  10.4 0.0 collective-permute-done.2.refs_3_
  10.4 0.0 copy-start
  10.4 0.0 copy-start.1
  10.4 0.0 copy-start.2
  10.4 2.6 %shard_map.84 = (bf16[272,256]{1,0:T(8,128)(2,1)S(1)}, bf16[8,128,128]{2,1,0:T(8,128)(2,1)S(1)}, f32[8,128,128]{2,1,0:T(8,128)S(1)}, f32[8,128]{1,0:T(8,128)S(1)}) custom-call(bf16[400,128]{1,0:T(8,128)(2,1)S(1)} %get-tuple-element.33.refs_0_, bf16[400,128]{1,0:T(8,128)(2,1)S(1)} %collective-permute-done.refs_1_, ...), custom_call_target="tpu_custom_call" | custom-call | flops 1073741824 | bytes 1048576 | tf_op jit(solution)/shard_map/pallas_call | solution.py:462
  13.1 1.6 %collective-permute-start.3 = (bf16[272,256]{1,0:T(8,128)(2,1)S(1)}, bf16[272,256]{1,0:T(8,128)(2,1)S(1)}, u32[]{:S(2)}, u32[]{:S(2)}) collective-permute-start(bf16[272,256]{1,0:T(8,128)(2,1)S(1)} %get-tuple-element.40.refs_5_.refs_0_), channel_id=1, source_target_pairs={{0,8},{2,10},{4,12},{6,14},{8,0},{10,2},{12,4},{14,6},{16,24},{18,... | collective-permute-start | bytes 417800 | tf_op jit(solution)/shard_map/ppermute | solution.py:422
  14.7 3.2 %shard_map.86 = (bf16[4,128,128]{2,1,0:T(8,128)(2,1)S(1)}, f32[4,128,128]{2,1,0:T(8,128)S(1)}) custom-call(bf16[128,512]{1,0:T(8,128)(2,1)} %refs_0_.6, bf16[128,512]{1,0:T(8,128)(2,1)} %refs_1_.5, bf16[128,1024]{1,0:T(8,128)(2,1)} %refs_2_.9, f32[8,128]{1,0:T(8,128)} %refs_3_.5, f32[8,128]{1,0:T(8,128)} %refs_4_.7, ...), custom_call_target="tpu_custom_call" | custom-call | flops 536870912 | bytes 1048576 | tf_op jit(solution)/shard_map/pallas_call | solution.py:449
  17.9 0.3 collective-permute-done.3.refs_3_.refs_1_
  18.2 0.2 shard_map.87
  18.4 2.7 %collective-permute-start.4 = (bf16[256,128]{1,0:T(8,128)(2,1)S(1)}, bf16[256,128]{1,0:T(8,128)(2,1)S(1)}, u32[]{:S(2)}, u32[]{:S(2)}) collective-permute-start(bf16[256,128]{1,0:T(8,128)(2,1)S(1)} %shard_map.87), channel_id=1, source_target_pairs={{0,16},{2,18},{4,20},{6,22},{8,24},{10,26},{12,28},{14,30},{16,0},... | collective-permute-start | bytes 196616 | tf_op jit(solution)/shard_map/ppermute | solution.py:422
  21.0 0.5 %shard_map.85 = (bf16[4,2,128,128]{3,2,1,0:T(8,128)(2,1)S(1)}, f32[4,2,128,128]{3,2,1,0:T(8,128)S(1)}) custom-call(bf16[8,128,128]{2,1,0:T(8,128)(2,1)S(1)} %get-tuple-element.37.refs_0_, f32[8,128,128]{2,1,0:T(8,128)S(1)} %get-tuple-element.38.refs_1_, f32[8,128]{1,0:T(8,128)S(1)} %get-tuple-element.39.refs_2_, ...), custom_call_target="tpu_custom_call" | custom-call | flops 268435456 | bytes 1048576 | tf_op jit(solution)/shard_map/pallas_call | solution.py:489
  21.6 2.0 %collective-permute-done.4.refs_2_ = bf16[256,128]{1,0:T(8,128)(2,1)S(1)} collective-permute-done((bf16[256,128]{1,0:T(8,128)(2,1)S(1)}, bf16[256,128]{1,0:T(8,128)(2,1)S(1)}, u32[]{:S(2)}, u32[]{:S(2)}) %collective-permute-start.4) | collective-permute-done | bytes 65568 | tf_op jit(solution)/shard_map/ppermute | solution.py:422
  23.6 0.2 shard_map.88
  23.8 1.9 %collective-permute-start.7 = (bf16[256,128]{1,0:T(8,128)(2,1)S(1)}, bf16[256,128]{1,0:T(8,128)(2,1)S(1)}, u32[]{:S(2)}, u32[]{:S(2)}) collective-permute-start(bf16[256,128]{1,0:T(8,128)(2,1)S(1)} %get-tuple-element.49), channel_id=1, source_target_pairs={{0,4},{1,3},{2,6},{3,1},{4,0},{5,7},{6,2},{7,5},{8,12},{9,11},{10,... | collective-permute-start | bytes 196616 | tf_op jit(solution)/shard_map/ppermute | solution.py:429
  25.7 0.6 %collective-permute-start.6 = (bf16[256,128]{1,0:T(8,128)(2,1)S(1)}, bf16[256,128]{1,0:T(8,128)(2,1)S(1)}, u32[]{:S(2)}, u32[]{:S(2)}) collective-permute-start(bf16[256,128]{1,0:T(8,128)(2,1)S(1)} %get-tuple-element.48), channel_id=1, source_target_pairs={{0,2},{1,5},{2,0},{3,7},{4,6},{5,1},{6,4},{7,3},{8,10},{9,13},{10,... | collective-permute-start | bytes 196616 | tf_op jit(solution)/shard_map/ppermute | solution.py:429
  26.3 1.1 %collective-permute-start.5 = (bf16[256,128]{1,0:T(8,128)(2,1)S(1)}, bf16[256,128]{1,0:T(8,128)(2,1)S(1)}, u32[]{:S(2)}, u32[]{:S(2)}) collective-permute-start(bf16[256,128]{1,0:T(8,128)(2,1)S(1)} %get-tuple-element.46), channel_id=1, source_target_pairs={{0,6},{1,7},{2,4},{3,5},{4,2},{5,3},{6,0},{7,1},{8,14},{9,15},{10,... | collective-permute-start | bytes 196616 | tf_op jit(solution)/shard_map/ppermute | solution.py:429
  27.4 0.0 copy-done
  27.4 0.0 copy-done.1
  27.4 0.0 copy-done.2
  27.4 0.4 %shard_map.89 = (f32[128,1024]{1,0:T(8,128)S(1)}, bf16[128,256]{1,0:T(8,128)(2,1)S(1)}) custom-call(bf16[4,128,128]{2,1,0:T(8,128)(2,1)S(1)} %get-tuple-element.31.refs_0_, f32[4,128,128]{2,1,0:T(8,128)S(1)} %get-tuple-element.32.refs_4_.refs_1_, bf16[128,1024]{1,0:T(8,128)(2,1)S(1)} %copy-done.1, f32[1,128]{1,0:T(1,128)S(1)} %bitcast.1, ...), custom_call_target="tpu_custom_call" | custom-call | flops 67108864 | bytes 1048576 | tf_op jit(solution)/shard_map/pallas_call | solution.py:510
  27.8 1.0 %collective-permute-done.7.refs_5_ = bf16[256,128]{1,0:T(8,128)(2,1)S(1)} collective-permute-done((bf16[256,128]{1,0:T(8,128)(2,1)S(1)}, bf16[256,128]{1,0:T(8,128)(2,1)S(1)}, u32[]{:S(2)}, u32[]{:S(2)}) %collective-permute-start.7) | collective-permute-done | bytes 65568 | tf_op jit(solution)/shard_map/ppermute | solution.py:429
  28.8 0.4 %shard_map.90 = (f32[128,1024]{1,0:T(8,128)S(1)}, bf16[128,256]{1,0:T(8,128)(2,1)S(1)}) custom-call(bf16[4,128,128]{2,1,0:T(8,128)(2,1)S(1)} %get-tuple-element.47.refs_0_, f32[4,128,128]{2,1,0:T(8,128)S(1)} %get-tuple-element.43.refs_2_.refs_1_, bf16[128,1024]{1,0:T(8,128)(2,1)S(1)} %copy-done.1, f32[1,128]{1,0:T(1,128)S(1)} %bitcast.2, ...), custom_call_target="tpu_custom_call" | custom-call | flops 67108864 | bytes 1048576 | tf_op jit(solution)/shard_map/pallas_call | solution.py:510
  29.3 0.7 %collective-permute-done.6.refs_5_ = bf16[256,128]{1,0:T(8,128)(2,1)S(1)} collective-permute-done((bf16[256,128]{1,0:T(8,128)(2,1)S(1)}, bf16[256,128]{1,0:T(8,128)(2,1)S(1)}, u32[]{:S(2)}, u32[]{:S(2)}) %collective-permute-start.6) | collective-permute-done | bytes 65568 | tf_op jit(solution)/shard_map/ppermute | solution.py:429
  30.0 0.4 %shard_map.91 = (f32[128,1024]{1,0:T(8,128)S(1)}, bf16[128,256]{1,0:T(8,128)(2,1)S(1)}) custom-call(bf16[4,128,128]{2,1,0:T(8,128)(2,1)S(1)} %get-tuple-element.47.refs_0_, f32[4,128,128]{2,1,0:T(8,128)S(1)} %get-tuple-element.43.refs_2_.refs_1_, bf16[128,1024]{1,0:T(8,128)(2,1)S(1)} %copy-done.1, f32[1,128]{1,0:T(1,128)S(1)} %bitcast.3, ...), custom_call_target="tpu_custom_call" | custom-call | flops 67108864 | bytes 1048576 | tf_op jit(solution)/shard_map/pallas_call | solution.py:510
  30.4 1.0 %collective-permute-done.5.refs_5_ = bf16[256,128]{1,0:T(8,128)(2,1)S(1)} collective-permute-done((bf16[256,128]{1,0:T(8,128)(2,1)S(1)}, bf16[256,128]{1,0:T(8,128)(2,1)S(1)}, u32[]{:S(2)}, u32[]{:S(2)}) %collective-permute-start.5) | collective-permute-done | bytes 65568 | tf_op jit(solution)/shard_map/ppermute | solution.py:429
  31.4 0.4 %shard_map.92 = (bf16[128,1024]{1,0:T(8,128)(2,1)S(1)}, bf16[128,256]{1,0:T(8,128)(2,1)S(1)}) custom-call(bf16[4,128,128]{2,1,0:T(8,128)(2,1)S(1)} %get-tuple-element.31.refs_0_, f32[4,128,128]{2,1,0:T(8,128)S(1)} %get-tuple-element.32.refs_4_.refs_1_, bf16[128,1024]{1,0:T(8,128)(2,1)S(1)} %copy-done.1, f32[1,128]{1,0:T(1,128)S(1)} %bitcast.4, ...), custom_call_target="tpu_custom_call" | custom-call | flops 67108864 | bytes 1048576 | tf_op jit(solution)/shard_map/pallas_call | solution.py:510
  31.9 0.1 collective-permute-start.8
  31.9 0.5 %shard_map.93 = f32[128,1024]{1,0:T(8,128)S(1)} custom-call(bf16[1024,2048]{1,0:T(8,128)(2,1)S(1)} %copy-done, bf16[128,256]{1,0:T(8,128)(2,1)S(1)} %get-tuple-element.45.refs_1_, bf16[128,256]{1,0:T(8,128)(2,1)S(1)} %get-tuple-element.53.refs_2_, bf16[128,256]{1,0:T(8,128)(2,1)S(1)} %get-tuple-element.54.refs_3_, bf16[128,256]{1,0:T(8,128)(2,1)S(1)} %get-tuple-element.55.refs_4_), custom_call_target="tpu_custom_call" | custom-call | flops 268435456 | bytes 1048576 | tf_op jit(solution)/shard_map/pallas_call | solution.py:520
  32.5 1.0 %collective-permute-done.8 = bf16[128,1024]{1,0:T(8,128)(2,1)S(1)} collective-permute-done((bf16[128,1024]{1,0:T(8,128)(2,1)S(1)}, bf16[128,1024]{1,0:T(8,128)(2,1)S(1)}, u32[]{:S(2)}, u32[]{:S(2)}) %collective-permute-start.8) | collective-permute-done | bytes 262176 | tf_op jit(solution)/shard_map/ppermute | solution.py:519
  33.5 0.8 %add_convert_fusion = bf16[128,1024]{1,0:T(8,128)(2,1)} fusion(f32[128,1024]{1,0:T(8,128)S(1)} %shard_map.93, bf16[128,1024]{1,0:T(8,128)(2,1)S(1)} %collective-permute-done.8), kind=kLoop, calls=%fused_computation | loop fusion | flops 393216 | bytes 1048576 | tf_op jit(solution)/shard_map/convert_element_type | solution.py:523
Async XLA Ops:
  1.1 7.8 %collective-permute-start = (bf16[400,128]{1,0:T(8,128)(2,1)S(1)}, bf16[400,128]{1,0:T(8,128)(2,1)S(1)}, u32[]{:S(2)}, u32[]{:S(2)}) collective-permute-start(bf16[400,128]{1,0:T(8,128)(2,1)S(1)} %get-tuple-element.34), channel_id=1, source_target_pairs={{0,6},{1,7},{2,4},{3,5},{4,2},{5,3},{6,0},{7,1},{8,14},{9,15},{10,... | collective-permute-start | bytes 307208 | tf_op jit(solution)/shard_map/ppermute | solution.py:429
  5.1 5.4 %collective-permute-start.1 = (bf16[400,128]{1,0:T(8,128)(2,1)S(1)}, bf16[400,128]{1,0:T(8,128)(2,1)S(1)}, u32[]{:S(2)}, u32[]{:S(2)}) collective-permute-start(bf16[400,128]{1,0:T(8,128)(2,1)S(1)} %get-tuple-element.35), channel_id=1, source_target_pairs={{0,2},{1,5},{2,0},{3,7},{4,6},{5,1},{6,4},{7,3},{8,10},{9,13},{10,... | collective-permute-start | bytes 307208 | tf_op jit(solution)/shard_map/ppermute | solution.py:429
  5.6 4.8 %collective-permute-start.2 = (bf16[400,128]{1,0:T(8,128)(2,1)S(1)}, bf16[400,128]{1,0:T(8,128)(2,1)S(1)}, u32[]{:S(2)}, u32[]{:S(2)}) collective-permute-start(bf16[400,128]{1,0:T(8,128)(2,1)S(1)} %get-tuple-element.36), channel_id=1, source_target_pairs={{0,4},{1,3},{2,6},{3,1},{4,0},{5,7},{6,2},{7,5},{8,12},{9,11},{10,... | collective-permute-start | bytes 307208 | tf_op jit(solution)/shard_map/ppermute | solution.py:429
  10.4 16.9 %copy-start = (bf16[1024,2048]{1,0:T(8,128)(2,1)S(1)}, bf16[1024,2048]{1,0:T(8,128)(2,1)}, u32[]{:S(2)}) copy-start(bf16[1024,2048]{1,0:T(8,128)(2,1)} %refs_0_.7) | copy-start | bytes 12582916
  10.4 16.9 %copy-start.1 = (bf16[128,1024]{1,0:T(8,128)(2,1)S(1)}, bf16[128,1024]{1,0:T(8,128)(2,1)}, u32[]{:S(2)}) copy-start(bf16[128,1024]{1,0:T(8,128)(2,1)} %refs_2_.13) | copy-start | bytes 786436
  10.4 16.9 %copy-start.2 = (f32[128]{0:T(128)S(1)}, f32[128]{0:T(128)}, u32[]{:S(2)}) copy-start(f32[128]{0:T(128)} %param.14) | copy-start | bytes 1540
  13.1 5.1 %collective-permute-start.3 = (bf16[272,256]{1,0:T(8,128)(2,1)S(1)}, bf16[272,256]{1,0:T(8,128)(2,1)S(1)}, u32[]{:S(2)}, u32[]{:S(2)}) collective-permute-start(bf16[272,256]{1,0:T(8,128)(2,1)S(1)} %get-tuple-element.40.refs_5_.refs_0_), channel_id=1, source_target_pairs={{0,8},{2,10},{4,12},{6,14},{8,0},{10,2},{12,4},{14,6},{16,24},{18,... | collective-permute-start | bytes 417800 | tf_op jit(solution)/shard_map/ppermute | solution.py:422
  18.4 5.2 %collective-permute-start.4 = (bf16[256,128]{1,0:T(8,128)(2,1)S(1)}, bf16[256,128]{1,0:T(8,128)(2,1)S(1)}, u32[]{:S(2)}, u32[]{:S(2)}) collective-permute-start(bf16[256,128]{1,0:T(8,128)(2,1)S(1)} %shard_map.87), channel_id=1, source_target_pairs={{0,16},{2,18},{4,20},{6,22},{8,24},{10,26},{12,28},{14,30},{16,0},... | collective-permute-start | bytes 196616 | tf_op jit(solution)/shard_map/ppermute | solution.py:422
  23.8 5.0 %collective-permute-start.7 = (bf16[256,128]{1,0:T(8,128)(2,1)S(1)}, bf16[256,128]{1,0:T(8,128)(2,1)S(1)}, u32[]{:S(2)}, u32[]{:S(2)}) collective-permute-start(bf16[256,128]{1,0:T(8,128)(2,1)S(1)} %get-tuple-element.49), channel_id=1, source_target_pairs={{0,4},{1,3},{2,6},{3,1},{4,0},{5,7},{6,2},{7,5},{8,12},{9,11},{10,... | collective-permute-start | bytes 196616 | tf_op jit(solution)/shard_map/ppermute | solution.py:429
  25.7 4.3 %collective-permute-start.6 = (bf16[256,128]{1,0:T(8,128)(2,1)S(1)}, bf16[256,128]{1,0:T(8,128)(2,1)S(1)}, u32[]{:S(2)}, u32[]{:S(2)}) collective-permute-start(bf16[256,128]{1,0:T(8,128)(2,1)S(1)} %get-tuple-element.48), channel_id=1, source_target_pairs={{0,2},{1,5},{2,0},{3,7},{4,6},{5,1},{6,4},{7,3},{8,10},{9,13},{10,... | collective-permute-start | bytes 196616 | tf_op jit(solution)/shard_map/ppermute | solution.py:429
  26.3 5.2 %collective-permute-start.5 = (bf16[256,128]{1,0:T(8,128)(2,1)S(1)}, bf16[256,128]{1,0:T(8,128)(2,1)S(1)}, u32[]{:S(2)}, u32[]{:S(2)}) collective-permute-start(bf16[256,128]{1,0:T(8,128)(2,1)S(1)} %get-tuple-element.46), channel_id=1, source_target_pairs={{0,6},{1,7},{2,4},{3,5},{4,2},{5,3},{6,0},{7,1},{8,14},{9,15},{10,... | collective-permute-start | bytes 196616 | tf_op jit(solution)/shard_map/ppermute | solution.py:429
  31.9 1.6 %collective-permute-start.8 = (bf16[128,1024]{1,0:T(8,128)(2,1)S(1)}, bf16[128,1024]{1,0:T(8,128)(2,1)S(1)}, u32[]{:S(2)}, u32[]{:S(2)}) collective-permute-start(bf16[128,1024]{1,0:T(8,128)(2,1)S(1)} %get-tuple-element.56), channel_id=1, source_target_pairs={{0,1},{1,0},{2,3},{3,2},{4,5},{5,4},{6,7},{7,6},{8,9},{9,8},{10,11... | collective-permute-start | bytes 786440 | tf_op jit(solution)/shard_map/ppermute | solution.py:519

commit v3 on v1

--- a/solution.py
+++ b/solution.py
@@ -143,13 +143,21 @@
     return run
 
 
+def store_rates(out, rate_ref, decay_ref, rank, s, rep):
+    tokens = rate_ref.shape[1]
+    rows = [slot_rows(ref, rank, [s], rep) for ref in (rate_ref, decay_ref)]
+    terms = [t.astype(F32) for t in parts(jnp.concatenate(rows, axis=0))]
+    terms.append(jnp.zeros((PAD - 6 * rep, tokens), F32))
+    out[(rep + 1) * tokens :, :] = jnp.concatenate(terms, axis=0).astype(BF16)
+
+
 def pack_body(dk, dv, rep, group, where, k_in, v_in, rate_in, decay_in, *refs):
     slots = flips(group, where[1])
     *outs, rate_ref, decay_ref, sems = refs
     tokens = k_in.shape[0]
     rank = where[0]
     pairs = [(rate_in, rate_ref), (decay_in, decay_ref)]
-    for s, out in zip(slots, outs):
+    for s, out in zip(slots[1:], outs):
         at = pl.multiple_of((rank ^ s) * dk, dk)
         pairs.append((k_in.at[:, pl.ds(at, dk)], out.at[0:tokens, :]))
         for h in range(rep):
@@ -161,11 +169,8 @@
         copy.start()
     copies[0].wait()
     copies[1].wait()
-    for s, out in zip(slots, outs):
-        rows = [slot_rows(ref, rank, [s], rep) for ref in (rate_ref, decay_ref)]
-        terms = [t.astype(F32) for t in parts(jnp.concatenate(rows, axis=0))]
-        terms.append(jnp.zeros((PAD - 6 * rep, tokens), F32))
-        out[(rep + 1) * tokens :, :] = jnp.concatenate(terms, axis=0).astype(BF16)
+    for s, out in zip(slots[1:], outs):
+        store_rates(out, rate_ref, decay_ref, rank, s, rep)
     for copy in copies[2:]:
         copy.wait()
 
@@ -241,7 +246,7 @@
 
 def terms_body(dk, dv, rep, group, where, q_in, k_in, v_in, rate_in, decay_in, *refs):
     slots = flips(group, where[1])
-    x_ref, y_ref, q_ref, k_ref, v_ref, rate_ref, decay_ref, sems = refs
+    x_ref, y_ref, own_ref, q_ref, k_ref, v_ref, rate_ref, decay_ref, sems = refs
     tokens = k_in.shape[0]
     rank = where[0]
     pairs = [(rate_in, rate_ref), (decay_in, decay_ref), (k_in, k_ref), (v_in, v_ref), (q_in, q_ref)]
@@ -262,6 +267,11 @@
         at = pl.multiple_of(((rank ^ slots[n // rep]) * rep + n % rep) * dv, dv)
         values.append(v_ref[:, pl.ds(at, dv)].astype(F32))
     solved = solve_blocks(keys, values, sides, rep)
+    own_ref[0:tokens, :] = k_ref[:, pl.ds(pl.multiple_of(rank * dk, dk), dk)]
+    for h in range(rep):
+        at = pl.multiple_of((rank * rep + h) * dv, dv)
+        own_ref[(h + 1) * tokens : (h + 2) * tokens, :] = v_ref[:, pl.ds(at, dv)]
+    store_rates(own_ref, rate_ref, decay_ref, rank, 0, rep)
     copies[4].wait()
     queries = [key_block(q_ref, rank ^ s, dk) * dk**-0.5 for s in slots]
     dots = [dot_nt(query, key) for query, key in zip(queries, keys)]
@@ -436,14 +446,14 @@
     pack_shape = shape(((rep + 1) * tokens + PAD, dk), BF16)
     packs = call(
         placed(functools.partial(pack_body, dk, dv, rep, group), group),
-        [pack_shape] * group,
+        [pack_shape] * (group - 1),
         [hbm] * 4,
-        small + [pltpu.SemaphoreType.DMA((2 + (rep + 1) * group,))],
+        small + [pltpu.SemaphoreType.DMA((2 + (rep + 1) * (group - 1),))],
     )(k_in, v_in, rate_in, decay_in)
-    packs = swap_slots(packs, range(1, group))
-    x, y = call(
+    packs = swap_slots([None, *packs], range(1, group))
+    x, y, packs[0] = call(
         placed(functools.partial(terms_body, dk, dv, rep, group), group),
-        [shape((heads, tokens, dk), BF16), shape((heads, tokens, dv), F32)],
+        [shape((heads, tokens, dk), BF16), shape((heads, tokens, dv), F32), pack_shape],
         [hbm] * 5,
         [pltpu.VMEM(z.shape, BF16) for z in (queries, key_rows, values)]
         + small

time: 34.4 us -> 34.4 us (level)
  no operation moved by 1% of the time
where the time goes in v3:
time: 34.4 us; the launch traced here: 34.2 us
  starting transfers between devices  12.5 us (36%)
  Pallas kernels  10.6 us (31%)
  waiting for transfers between devices  10.2 us (30%)
  other arithmetic  0.76 us (2%)
    ppermute x6, starting transfers between devices, swap_slots(): came[n] = lax.ppermute(x, ('seq', 'head'), pairs)  8.15 us
    ppermute x2, waiting for transfers between devices, swap(): return lax.ppermute(x, 'seq', [(i, i ^ flip) for i in range(ranks)])  5.5 us
    ppermute x2, starting transfers between devices, swap(): return lax.ppermute(x, 'seq', [(i, i ^ flip) for i in range(ranks)])  4.3 us
    pallas_call x1, Pallas kernels, per_device(): call(placed(functools.partial(terms_body, dk, dv, rep, group), group), [s...  3.84 us
    ppermute x6, waiting for transfers between devices, swap_slots(): came[n] = lax.ppermute(x, ('seq', 'head'), pairs)  3.65 us
    pallas_call x1, Pallas kernels, per_device(): call(placed(functools.partial(owner_body, dk, dv, rep, group, steps > 1),...  2.61 us
    pallas_call x4, Pallas kernels, per_device(): call(placed(functools.partial(project_body, dk, dv, rep, group, n), group...  1.71 us
    pallas_call x1, Pallas kernels, per_device(): call(placed(functools.partial(pack_body, dk, dv, rep, group), group), [pa...  1.02 us
  transfers between devices with their start and end apart: 9, of which 7 were waited for; matrix products, arithmetic and copies ran while one was open for 0% of the time, Pallas kernels for 18%

profile of v3, /device:TPU:0, one launch (start us, length us, event | category | flops | bytes accessed | tf_op | source)
XLA Modules:
  0.0 34.2 jit_solution(12454150516573373492)
XLA Ops:
  0.0 1.0 %shard_map.83 = (bf16[400,128]{1,0:T(8,128)(2,1)S(1)}, bf16[400,128]{1,0:T(8,128)(2,1)S(1)}, bf16[400,128]{1,0:T(8,128)(2,1)S(1)}) custom-call(bf16[128,512]{1,0:T(8,128)(2,1)} %refs_0_.4, bf16[128,1024]{1,0:T(8,128)(2,1)} %refs_1_.3, f32[8,128]{1,0:T(8,128)} %refs_2_.7, f32[8,128]{1,0:T(8,128)} %refs_3_.3), custom_call_target="tpu_custom_call" | custom-call | bytes 1048576 | tf_op jit(solution)/shard_map/pallas_call | solution.py:447
  1.0 4.0 %collective-permute-start = (bf16[400,128]{1,0:T(8,128)(2,1)S(1)}, bf16[400,128]{1,0:T(8,128)(2,1)S(1)}, u32[]{:S(2)}, u32[]{:S(2)}) collective-permute-start(bf16[400,128]{1,0:T(8,128)(2,1)S(1)} %get-tuple-element.32), channel_id=1, source_target_pairs={{0,6},{1,7},{2,4},{3,5},{4,2},{5,3},{6,0},{7,1},{8,14},{9,15},{10,... | collective-permute-start | bytes 307208 | tf_op jit(solution)/shard_map/ppermute | solution.py:438
  5.0 0.5 %collective-permute-start.1 = (bf16[400,128]{1,0:T(8,128)(2,1)S(1)}, bf16[400,128]{1,0:T(8,128)(2,1)S(1)}, u32[]{:S(2)}, u32[]{:S(2)}) collective-permute-start(bf16[400,128]{1,0:T(8,128)(2,1)S(1)} %get-tuple-element.33), channel_id=1, source_target_pairs={{0,2},{1,5},{2,0},{3,7},{4,6},{5,1},{6,4},{7,3},{8,10},{9,13},{10,... | collective-permute-start | bytes 307208 | tf_op jit(solution)/shard_map/ppermute | solution.py:438
  5.5 0.0 copy-start
  5.5 0.0 copy-start.1
  5.5 0.0 copy-start.2
  5.5 0.1 collective-permute-start.2
  5.6 3.8 %shard_map.82 = (bf16[8,128,128]{2,1,0:T(8,128)(2,1)S(1)}, f32[8,128,128]{2,1,0:T(8,128)S(1)}, bf16[400,128]{1,0:T(8,128)(2,1)S(1)}) custom-call(bf16[128,512]{1,0:T(8,128)(2,1)} %refs_0_.3, bf16[128,512]{1,0:T(8,128)(2,1)} %refs_0_.4, bf16[128,1024]{1,0:T(8,128)(2,1)} %refs_1_.3, f32[8,128]{1,0:T(8,128)} %refs_2_.7, f32[8,128]{1,0:T(8,128)} %refs_3_.3), custom_call_target="tpu_custom_call" | custom-call | flops 1073741824 | bytes 1048576 | tf_op jit(solution)/shard_map/pallas_call | solution.py:454
  9.5 0.0 collective-permute-done.refs_1_
  9.5 0.9 %collective-permute-done.1.refs_2_ = bf16[400,128]{1,0:T(8,128)(2,1)S(1)} collective-permute-done((bf16[400,128]{1,0:T(8,128)(2,1)S(1)}, bf16[400,128]{1,0:T(8,128)(2,1)S(1)}, u32[]{:S(2)}, u32[]{:S(2)}) %collective-permute-start.1) | collective-permute-done | bytes 102432 | tf_op jit(solution)/shard_map/ppermute | solution.py:438
  10.4 0.0 collective-permute-done.2.refs_3_
  10.4 2.6 %shard_map.84 = (bf16[272,256]{1,0:T(8,128)(2,1)S(1)}, bf16[8,128,128]{2,1,0:T(8,128)(2,1)S(1)}, f32[8,128,128]{2,1,0:T(8,128)S(1)}, f32[8,128]{1,0:T(8,128)S(1)}) custom-call(bf16[400,128]{1,0:T(8,128)(2,1)S(1)} %get-tuple-element.31.refs_0_, bf16[400,128]{1,0:T(8,128)(2,1)S(1)} %collective-permute-done.refs_1_, ...), custom_call_target="tpu_custom_call" | custom-call | flops 1073741824 | bytes 1048576 | tf_op jit(solution)/shard_map/pallas_call | solution.py:464
  13.0 1.6 %collective-permute-start.3 = (bf16[272,256]{1,0:T(8,128)(2,1)S(1)}, bf16[272,256]{1,0:T(8,128)(2,1)S(1)}, u32[]{:S(2)}, u32[]{:S(2)}) collective-permute-start(bf16[272,256]{1,0:T(8,128)(2,1)S(1)} %get-tuple-element.38.refs_0_), channel_id=1, source_target_pairs={{0,8},{2,10},{4,12},{6,14},{8,0},{10,2},{12,4},{14,6},{16,24},{18,... | collective-permute-start | bytes 417800 | tf_op jit(solution)/shard_map/ppermute | solution.py:431
  14.6 3.5 %collective-permute-done.3.refs_3_.refs_1_ = bf16[272,256]{1,0:T(8,128)(2,1)S(1)} collective-permute-done((bf16[272,256]{1,0:T(8,128)(2,1)S(1)}, bf16[272,256]{1,0:T(8,128)(2,1)S(1)}, u32[]{:S(2)}, u32[]{:S(2)}) %collective-permute-start.3) | collective-permute-done | bytes 139296 | tf_op jit(solution)/shard_map/ppermute | solution.py:431
  18.1 0.2 shard_map.86
  18.3 2.7 %collective-permute-start.4 = (bf16[256,128]{1,0:T(8,128)(2,1)S(1)}, bf16[256,128]{1,0:T(8,128)(2,1)S(1)}, u32[]{:S(2)}, u32[]{:S(2)}) collective-permute-start(bf16[256,128]{1,0:T(8,128)(2,1)S(1)} %shard_map.86), channel_id=1, source_target_pairs={{0,16},{2,18},{4,20},{6,22},{8,24},{10,26},{12,28},{14,30},{16,0},... | collective-permute-start | bytes 196616 | tf_op jit(solution)/shard_map/ppermute | solution.py:431
  20.9 0.5 %shard_map.85 = (bf16[4,2,128,128]{3,2,1,0:T(8,128)(2,1)S(1)}, f32[4,2,128,128]{3,2,1,0:T(8,128)S(1)}) custom-call(bf16[8,128,128]{2,1,0:T(8,128)(2,1)S(1)} %get-tuple-element.35.refs_0_, f32[8,128,128]{2,1,0:T(8,128)S(1)} %get-tuple-element.36.refs_1_, f32[8,128]{1,0:T(8,128)S(1)} %get-tuple-element.37.refs_2_, ...), custom_call_target="tpu_custom_call" | custom-call | flops 268435456 | bytes 1048576 | tf_op jit(solution)/shard_map/pallas_call | solution.py:490
  21.5 2.0 %collective-permute-done.4.refs_2_ = bf16[256,128]{1,0:T(8,128)(2,1)S(1)} collective-permute-done((bf16[256,128]{1,0:T(8,128)(2,1)S(1)}, bf16[256,128]{1,0:T(8,128)(2,1)S(1)}, u32[]{:S(2)}, u32[]{:S(2)}) %collective-permute-start.4) | collective-permute-done | bytes 65568 | tf_op jit(solution)/shard_map/ppermute | solution.py:431
  23.5 0.2 shard_map.87
  23.7 1.9 %collective-permute-start.7 = (bf16[256,128]{1,0:T(8,128)(2,1)S(1)}, bf16[256,128]{1,0:T(8,128)(2,1)S(1)}, u32[]{:S(2)}, u32[]{:S(2)}) collective-permute-start(bf16[256,128]{1,0:T(8,128)(2,1)S(1)} %get-tuple-element.45), channel_id=1, source_target_pairs={{0,4},{1,3},{2,6},{3,1},{4,0},{5,7},{6,2},{7,5},{8,12},{9,11},{10,... | collective-permute-start | bytes 196616 | tf_op jit(solution)/shard_map/ppermute | solution.py:438
  25.6 0.6 %collective-permute-start.6 = (bf16[256,128]{1,0:T(8,128)(2,1)S(1)}, bf16[256,128]{1,0:T(8,128)(2,1)S(1)}, u32[]{:S(2)}, u32[]{:S(2)}) collective-permute-start(bf16[256,128]{1,0:T(8,128)(2,1)S(1)} %get-tuple-element.44), channel_id=1, source_target_pairs={{0,2},{1,5},{2,0},{3,7},{4,6},{5,1},{6,4},{7,3},{8,10},{9,13},{10,... | collective-permute-start | bytes 196616 | tf_op jit(solution)/shard_map/ppermute | solution.py:438
  26.2 1.1 %collective-permute-start.5 = (bf16[256,128]{1,0:T(8,128)(2,1)S(1)}, bf16[256,128]{1,0:T(8,128)(2,1)S(1)}, u32[]{:S(2)}, u32[]{:S(2)}) collective-permute-start(bf16[256,128]{1,0:T(8,128)(2,1)S(1)} %get-tuple-element.43), channel_id=1, source_target_pairs={{0,6},{1,7},{2,4},{3,5},{4,2},{5,3},{6,0},{7,1},{8,14},{9,15},{10,... | collective-permute-start | bytes 196616 | tf_op jit(solution)/shard_map/ppermute | solution.py:438
  27.3 0.0 copy-done
  27.3 0.0 copy-done.1
  27.3 0.0 copy-done.2
  27.3 0.4 %shard_map.88 = (f32[128,1024]{1,0:T(8,128)S(1)}, bf16[128,256]{1,0:T(8,128)(2,1)S(1)}) custom-call(bf16[8,128,128]{2,1,0:T(8,128)(2,1)S(1)} %get-tuple-element.29.refs_0_, f32[8,128,128]{2,1,0:T(8,128)S(1)} %get-tuple-element.30.refs_4_.refs_1_, bf16[128,1024]{1,0:T(8,128)(2,1)S(1)} %copy-done.1, f32[1,128]{1,0:T(1,128)S(1)} %bitcast.1, ...), custom_call_target="tpu_custom_call" | custom-call | flops 67108864 | bytes 1048576 | tf_op jit(solution)/shard_map/pallas_call | solution.py:511
  27.7 1.0 %collective-permute-done.7.refs_5_ = bf16[256,128]{1,0:T(8,128)(2,1)S(1)} collective-permute-done((bf16[256,128]{1,0:T(8,128)(2,1)S(1)}, bf16[256,128]{1,0:T(8,128)(2,1)S(1)}, u32[]{:S(2)}, u32[]{:S(2)}) %collective-permute-start.7) | collective-permute-done | bytes 65568 | tf_op jit(solution)/shard_map/ppermute | solution.py:438
  28.8 0.4 %shard_map.89 = (f32[128,1024]{1,0:T(8,128)S(1)}, bf16[128,256]{1,0:T(8,128)(2,1)S(1)}) custom-call(bf16[8,128,128]{2,1,0:T(8,128)(2,1)S(1)} %get-tuple-element.29.refs_0_, f32[8,128,128]{2,1,0:T(8,128)S(1)} %get-tuple-element.30.refs_4_.refs_1_, bf16[128,1024]{1,0:T(8,128)(2,1)S(1)} %copy-done.1, f32[1,128]{1,0:T(1,128)S(1)} %bitcast.2, ...), custom_call_target="tpu_custom_call" | custom-call | flops 67108864 | bytes 1048576 | tf_op jit(solution)/shard_map/pallas_call | solution.py:511
  29.2 0.7 %collective-permute-done.6.refs_5_ = bf16[256,128]{1,0:T(8,128)(2,1)S(1)} collective-permute-done((bf16[256,128]{1,0:T(8,128)(2,1)S(1)}, bf16[256,128]{1,0:T(8,128)(2,1)S(1)}, u32[]{:S(2)}, u32[]{:S(2)}) %collective-permute-start.6) | collective-permute-done | bytes 65568 | tf_op jit(solution)/shard_map/ppermute | solution.py:438
  29.9 0.4 %shard_map.90 = (f32[128,1024]{1,0:T(8,128)S(1)}, bf16[128,256]{1,0:T(8,128)(2,1)S(1)}) custom-call(bf16[8,128,128]{2,1,0:T(8,128)(2,1)S(1)} %get-tuple-element.29.refs_0_, f32[8,128,128]{2,1,0:T(8,128)S(1)} %get-tuple-element.30.refs_4_.refs_1_, bf16[128,1024]{1,0:T(8,128)(2,1)S(1)} %copy-done.1, f32[1,128]{1,0:T(1,128)S(1)} %bitcast.3, ...), custom_call_target="tpu_custom_call" | custom-call | flops 67108864 | bytes 1048576 | tf_op jit(solution)/shard_map/pallas_call | solution.py:511
  30.3 1.1 %collective-permute-done.5.refs_5_ = bf16[256,128]{1,0:T(8,128)(2,1)S(1)} collective-permute-done((bf16[256,128]{1,0:T(8,128)(2,1)S(1)}, bf16[256,128]{1,0:T(8,128)(2,1)S(1)}, u32[]{:S(2)}, u32[]{:S(2)}) %collective-permute-start.5) | collective-permute-done | bytes 65568 | tf_op jit(solution)/shard_map/ppermute | solution.py:438
  31.4 0.4 %shard_map.91 = (bf16[128,1024]{1,0:T(8,128)(2,1)S(1)}, bf16[128,256]{1,0:T(8,128)(2,1)S(1)}) custom-call(bf16[8,128,128]{2,1,0:T(8,128)(2,1)S(1)} %get-tuple-element.29.refs_0_, f32[8,128,128]{2,1,0:T(8,128)S(1)} %get-tuple-element.30.refs_4_.refs_1_, bf16[128,1024]{1,0:T(8,128)(2,1)S(1)} %copy-done.1, f32[1,128]{1,0:T(1,128)S(1)} %bitcast.4, ...), custom_call_target="tpu_custom_call" | custom-call | flops 67108864 | bytes 1048576 | tf_op jit(solution)/shard_map/pallas_call | solution.py:511
  31.8 0.1 collective-permute-start.8
  31.9 0.5 %shard_map.92 = f32[128,1024]{1,0:T(8,128)S(1)} custom-call(bf16[1024,2048]{1,0:T(8,128)(2,1)S(1)} %copy-done, bf16[128,256]{1,0:T(8,128)(2,1)S(1)} %get-tuple-element.42.refs_1_, bf16[128,256]{1,0:T(8,128)(2,1)S(1)} %get-tuple-element.49.refs_2_, bf16[128,256]{1,0:T(8,128)(2,1)S(1)} %get-tuple-element.50.refs_3_, bf16[128,256]{1,0:T(8,128)(2,1)S(1)} %get-tuple-element.51.refs_4_), custom_call_target="tpu_custom_call" | custom-call | flops 268435456 | bytes 1048576 | tf_op jit(solution)/shard_map/pallas_call | solution.py:521
  32.4 1.0 %collective-permute-done.8 = bf16[128,1024]{1,0:T(8,128)(2,1)S(1)} collective-permute-done((bf16[128,1024]{1,0:T(8,128)(2,1)S(1)}, bf16[128,1024]{1,0:T(8,128)(2,1)S(1)}, u32[]{:S(2)}, u32[]{:S(2)}) %collective-permute-start.8) | collective-permute-done | bytes 262176 | tf_op jit(solution)/shard_map/ppermute | solution.py:520
  33.4 0.8 %add_convert_fusion = bf16[128,1024]{1,0:T(8,128)(2,1)} fusion(f32[128,1024]{1,0:T(8,128)S(1)} %shard_map.92, bf16[128,1024]{1,0:T(8,128)(2,1)S(1)} %collective-permute-done.8), kind=kLoop, calls=%fused_computation | loop fusion | flops 393216 | bytes 1048576 | tf_op jit(solution)/shard_map/convert_element_type | solution.py:524
Async XLA Ops:
  1.0 8.5 %collective-permute-start = (bf16[400,128]{1,0:T(8,128)(2,1)S(1)}, bf16[400,128]{1,0:T(8,128)(2,1)S(1)}, u32[]{:S(2)}, u32[]{:S(2)}) collective-permute-start(bf16[400,128]{1,0:T(8,128)(2,1)S(1)} %get-tuple-element.32), channel_id=1, source_target_pairs={{0,6},{1,7},{2,4},{3,5},{4,2},{5,3},{6,0},{7,1},{8,14},{9,15},{10,... | collective-permute-start | bytes 307208 | tf_op jit(solution)/shard_map/ppermute | solution.py:438
  5.0 5.4 %collective-permute-start.1 = (bf16[400,128]{1,0:T(8,128)(2,1)S(1)}, bf16[400,128]{1,0:T(8,128)(2,1)S(1)}, u32[]{:S(2)}, u32[]{:S(2)}) collective-permute-start(bf16[400,128]{1,0:T(8,128)(2,1)S(1)} %get-tuple-element.33), channel_id=1, source_target_pairs={{0,2},{1,5},{2,0},{3,7},{4,6},{5,1},{6,4},{7,3},{8,10},{9,13},{10,... | collective-permute-start | bytes 307208 | tf_op jit(solution)/shard_map/ppermute | solution.py:438
  5.5 21.8 %copy-start = (bf16[1024,2048]{1,0:T(8,128)(2,1)S(1)}, bf16[1024,2048]{1,0:T(8,128)(2,1)}, u32[]{:S(2)}) copy-start(bf16[1024,2048]{1,0:T(8,128)(2,1)} %refs_0_.5) | copy-start | bytes 12582916
  5.5 21.8 %copy-start.1 = (bf16[128,1024]{1,0:T(8,128)(2,1)S(1)}, bf16[128,1024]{1,0:T(8,128)(2,1)}, u32[]{:S(2)}) copy-start(bf16[128,1024]{1,0:T(8,128)(2,1)} %refs_2_.11) | copy-start | bytes 786436
  5.5 21.8 %copy-start.2 = (f32[128]{0:T(128)S(1)}, f32[128]{0:T(128)}, u32[]{:S(2)}) copy-start(f32[128]{0:T(128)} %param.14) | copy-start | bytes 1540
  5.5 4.8 %collective-permute-start.2 = (bf16[400,128]{1,0:T(8,128)(2,1)S(1)}, bf16[400,128]{1,0:T(8,128)(2,1)S(1)}, u32[]{:S(2)}, u32[]{:S(2)}) collective-permute-start(bf16[400,128]{1,0:T(8,128)(2,1)S(1)} %get-tuple-element.34), channel_id=1, source_target_pairs={{0,4},{1,3},{2,6},{3,1},{4,0},{5,7},{6,2},{7,5},{8,12},{9,11},{10,... | collective-permute-start | bytes 307208 | tf_op jit(solution)/shard_map/ppermute | solution.py:438
  13.0 5.1 %collective-permute-start.3 = (bf16[272,256]{1,0:T(8,128)(2,1)S(1)}, bf16[272,256]{1,0:T(8,128)(2,1)S(1)}, u32[]{:S(2)}, u32[]{:S(2)}) collective-permute-start(bf16[272,256]{1,0:T(8,128)(2,1)S(1)} %get-tuple-element.38.refs_0_), channel_id=1, source_target_pairs={{0,8},{2,10},{4,12},{6,14},{8,0},{10,2},{12,4},{14,6},{16,24},{18,... | collective-permute-start | bytes 417800 | tf_op jit(solution)/shard_map/ppermute | solution.py:431
  18.3 5.2 %collective-permute-start.4 = (bf16[256,128]{1,0:T(8,128)(2,1)S(1)}, bf16[256,128]{1,0:T(8,128)(2,1)S(1)}, u32[]{:S(2)}, u32[]{:S(2)}) collective-permute-start(bf16[256,128]{1,0:T(8,128)(2,1)S(1)} %shard_map.86), channel_id=1, source_target_pairs={{0,16},{2,18},{4,20},{6,22},{8,24},{10,26},{12,28},{14,30},{16,0},... | collective-permute-start | bytes 196616 | tf_op jit(solution)/shard_map/ppermute | solution.py:431
  23.7 5.0 %collective-permute-start.7 = (bf16[256,128]{1,0:T(8,128)(2,1)S(1)}, bf16[256,128]{1,0:T(8,128)(2,1)S(1)}, u32[]{:S(2)}, u32[]{:S(2)}) collective-permute-start(bf16[256,128]{1,0:T(8,128)(2,1)S(1)} %get-tuple-element.45), channel_id=1, source_target_pairs={{0,4},{1,3},{2,6},{3,1},{4,0},{5,7},{6,2},{7,5},{8,12},{9,11},{10,... | collective-permute-start | bytes 196616 | tf_op jit(solution)/shard_map/ppermute | solution.py:438
  25.6 4.3 %collective-permute-start.6 = (bf16[256,128]{1,0:T(8,128)(2,1)S(1)}, bf16[256,128]{1,0:T(8,128)(2,1)S(1)}, u32[]{:S(2)}, u32[]{:S(2)}) collective-permute-start(bf16[256,128]{1,0:T(8,128)(2,1)S(1)} %get-tuple-element.44), channel_id=1, source_target_pairs={{0,2},{1,5},{2,0},{3,7},{4,6},{5,1},{6,4},{7,3},{8,10},{9,13},{10,... | collective-permute-start | bytes 196616 | tf_op jit(solution)/shard_map/ppermute | solution.py:438
  26.2 5.2 %collective-permute-start.5 = (bf16[256,128]{1,0:T(8,128)(2,1)S(1)}, bf16[256,128]{1,0:T(8,128)(2,1)S(1)}, u32[]{:S(2)}, u32[]{:S(2)}) collective-permute-start(bf16[256,128]{1,0:T(8,128)(2,1)S(1)} %get-tuple-element.43), channel_id=1, source_target_pairs={{0,6},{1,7},{2,4},{3,5},{4,2},{5,3},{6,0},{7,1},{8,14},{9,15},{10,... | collective-permute-start | bytes 196616 | tf_op jit(solution)/shard_map/ppermute | solution.py:438
  31.8 1.6 %collective-permute-start.8 = (bf16[128,1024]{1,0:T(8,128)(2,1)S(1)}, bf16[128,1024]{1,0:T(8,128)(2,1)S(1)}, u32[]{:S(2)}, u32[]{:S(2)}) collective-permute-start(bf16[128,1024]{1,0:T(8,128)(2,1)S(1)} %get-tuple-element.52), channel_id=1, source_target_pairs={{0,1},{1,0},{2,3},{3,2},{4,5},{5,4},{6,7},{7,6},{8,9},{9,8},{10,11... | collective-permute-start | bytes 786440 | tf_op jit(solution)/shard_map/ppermute | solution.py:520
